TPU v7x, 128 devices: a whole 4x4x4 slice. The times are simulated.
128 devices in a mesh: replica: 8 (over y_hi, z), tensor: 16 (over x, y_lo, core).
Axes of the slice: x: 4, y: 4 (y_hi: 2, y_lo: 2; y = y_hi * 2 + y_lo), z: 4, core: 2. Of those that a mesh axis runs over, the one named last changes fastest.
Arguments:
- features: bfloat16 [1536, 3, 8192], P('replica', None, 'tensor'), may hold values from -6 to 6
- accepted: int32 [8], P('replica'), may hold values from 96 to 192
- owner: int32 [1536, 1], P('replica'), may hold values from 0 to 15; in each aligned block of 1536 rows (0 to 1535, 1536 to 3071, ...) at most 192 rows name the same one
- draft_ids: int32 [1536], P('replica'), may hold values from 0 to 31999
- fc_weight: bfloat16 [3, 8192, 8192], P(None, 'tensor', 'replica'), may hold values from -0.0390625 to 0.0390625
- embed_table: bfloat16 [32000, 8192], P('tensor', 'replica'), may hold values from -6 to 6
- embed_gain: float32 [8192], P('replica'), may hold values from 0.1 to 1.9
- hidden_gain: float32 [8192], P('replica'), may hold values from 0.1 to 1.9
- hidden_grad: bfloat16 [3072, 8192], P('tensor', 'replica'), may hold values from -6 to 6
Outputs:
- draft_input: bfloat16 [3072, 2, 8192], P('tensor', None, 'replica')
- grad_fc: float32 [3, 8192, 8192], P(None, 'tensor', 'replica')
Inputs may be any that keep to these rules, and one draw needn't show every extreme that they name: Over all 1536 rows no owner is named by more than 192 rows, a bound that some block reaches.
All inputs are finite; a program needn't handle non-finite values.
Results may differ from a plain program's by a relative error of at most 0.0029.
Values may be sent and summed in bfloat16 or wider, within the bound.
No kernel may reach another device: no remote copies, remote signals or barrier semaphores. Data moves between devices by JAX's collectives and lax.ppermute only.
A program may use at most 128 MiB of HBM per device.

v0:
```python
import jax
import jax.numpy as jnp
from jax import lax
from jax.sharding import PartitionSpec as P

D = 8192
TAPS = 3


EPSILON = 1e-05


def slot_layout(accepted, owners, per_server, capacity, owner_count):
    row_total = owners.shape[0]
    row_index = jnp.arange(row_total, dtype=jnp.int32)
    limits = jnp.repeat(accepted, per_server, total_repeat_length=row_total)
    valid = row_index % per_server < limits
    picks = (
        (owners[:, None] == jnp.arange(owner_count, dtype=jnp.int32)[None, :]) & valid[:, None]
    ).astype(jnp.int32)
    before = jnp.cumsum(picks, axis=0) - picks
    ranking = jnp.sum(before * picks, axis=1)
    slot_total = owner_count * capacity
    target = jnp.where(valid, owners * capacity + ranking, slot_total).astype(jnp.int32)
    source = jnp.zeros((slot_total,), jnp.int32).at[target].set(row_index, mode="drop")
    filled = jnp.zeros((slot_total,), jnp.int32).at[target].set(1, mode="drop")
    return (valid, target, source, filled)


def body(
    features,
    accepted,
    owner,
    draft_ids,
    fc_weight,
    embed_table,
    embed_gain,
    hidden_gain,
    hidden_grad,
):
    owner_count = lax.axis_size("tensor")
    tensor_index = lax.axis_index("tensor")
    per_server = features.shape[0]
    capacity = hidden_grad.shape[0]
    feat_width = features.shape[2]
    col_width = fc_weight.shape[2]
    all_feats, all_ids, all_owner, all_accepted = (
        lax.all_gather(features, "replica", axis=0, tiled=True),
        lax.all_gather(draft_ids, "replica", axis=0, tiled=True),
        lax.all_gather(owner, "replica", axis=0, tiled=True),
        lax.all_gather(accepted, "replica", axis=0, tiled=True),
    )
    row_total = all_feats.shape[0]
    owners_flat = all_owner[:, 0]
    valid, target, source, filled = slot_layout(
        all_accepted, owners_flat, per_server, capacity, owner_count
    )
    row_feats = all_feats.reshape(row_total, TAPS * feat_width)
    weight_rows = fc_weight.reshape(TAPS * feat_width, col_width)
    vocab_local = embed_table.shape[0]
    local_ids = all_ids - tensor_index * vocab_local
    in_shard = (local_ids >= 0) & (local_ids < vocab_local)
    embed_rows = jnp.where(
        in_shard[:, None],
        embed_table[jnp.clip(local_ids, 0, vocab_local - 1)],
        jnp.zeros((), jnp.bfloat16),
    )
    my_filled = (lax.dynamic_slice_in_dim(filled, tensor_index * capacity, capacity) > 0)[:, None]
    picked = source
    present = (filled > 0)[:, None]
    chosen = jnp.where(present, row_feats[picked], jnp.zeros((), jnp.bfloat16))
    product = jnp.dot(chosen, weight_rows, preferred_element_type=jnp.float32)
    looked = jnp.where(present, embed_rows[picked].astype(jnp.float32), jnp.float32(0.0))
    summed = lax.psum_scatter(
        jnp.stack([looked, product], axis=1), "tensor", scatter_dimension=0, tiled=True
    )
    embeds = summed[:, 0]
    united = summed[:, 1]
    weighted = jnp.where(my_filled, hidden_grad.astype(jnp.float32) * hidden_gain, jnp.float32(0.0))
    squares = jnp.stack(
        [jnp.sum(united * united, axis=1), jnp.sum(embeds * embeds, axis=1)], axis=1
    )
    total_squares = lax.psum(squares, "replica")
    r_hidden = lax.rsqrt(total_squares[:, 0:1] / D + EPSILON)
    r_embed = lax.rsqrt(total_squares[:, 1:2] / D + EPSILON)
    normed = united * r_hidden
    normed_inner = lax.psum(jnp.sum(normed * weighted, axis=1), "replica")
    united_grad = (r_hidden * (weighted - normed * normed_inner[:, None] / D)).astype(jnp.bfloat16)
    draft_input = jnp.stack(
        [embeds * r_embed * embed_gain, united * r_hidden * hidden_gain], axis=1
    ).astype(jnp.bfloat16)
    start_value = jnp.zeros((TAPS * feat_width, col_width), jnp.float32)
    shard_rows = lax.all_gather(united_grad, "tensor", axis=0, tiled=True)
    length = shard_rows.shape[0]
    picked = lax.slice_in_dim(source, 0, length, axis=0)
    present = (lax.slice_in_dim(filled, 0, length, axis=0) > 0)[:, None]
    chosen = jnp.where(present, row_feats[picked], jnp.zeros((), jnp.bfloat16))
    folded = start_value + lax.dot_general(
        chosen, shard_rows, (((0,), (0,)), ((), ())), preferred_element_type=jnp.float32
    )
    grad_fc = folded.reshape(TAPS, feat_width, col_width)
    return (draft_input, grad_fc)


def solution(mesh):
    return jax.shard_map(
        body,
        mesh=mesh,
        in_specs=(
            P("replica", None, "tensor"),
            P("replica"),
            P("replica", None),
            P("replica"),
            P(None, "tensor", "replica"),
            P("tensor", "replica"),
            P("replica"),
            P("replica"),
            P("tensor", "replica"),
        ),
        out_specs=(P("tensor", None, "replica"), P(None, "tensor", "replica")),
        check_vma=False,
    )
```

profile of v0, /device:TPU:0, one launch (start us, length us, event | category | flops | bytes accessed | tf_op | source)
XLA Modules:
  0.0 569.9 jit_solution(783276418954710630)
XLA Ops:
  7.2 0.7 all-gather.3.cloned.1.call-update
  8.8 1.2 dynamic-slice.6
  10.7 0.9 dynamic-update-slice.4
  11.6 0.9 dynamic-update-slice.5
  12.4 0.8 dynamic-update-slice.3
  13.2 43.5 %all-reduce.3 = (s32[1536]{0:T(1024)S(1)}, s32[8]{0:T(128)S(1)}, s32[1536]{0:T(1024)S(1)}) all-reduce(s32[1536]{0:T(1024)S(1)} %dynamic-update-slice.4, s32[8]{0:T(128)S(1)} %dynamic-update-slice.3, s32[1536]{0:T(1024)S(1)} %dynamic-update-slice.5), channel_id=1, replica_groups=mesh['replica'=8,'tensor'=16] {'replica'}, use_global_device_ids=true, to_apply=%add.1 | all-reduce | flops 3080 | bytes 24640
  57.4 5.8 %fusion.10 = pred[12,128]{1,0:T(8,128)(4,1)S(1)} fusion(pred[1536]{0:T(1024)(128)(4,1)} %constant.173, pred[1536]{0:T(1024)(128)(4,1)} %constant.174, pred[1536]{0:T(1024)(128)(4,1)} %constant.175, pred[1536]{0:T(1024)(128)(4,1)} %constant.176, pred[1536]{0:T(1024)(128)(4,1)} %constant.177, pred[1536]{0:T(1024)(128)(4,1)} %constant.178, ...), kind=kLoop, calls=%fused_computation.41 | loop fusion | flops 24576 | bytes 12320 | tf_op jit(solution)/shard_map/lt | solution.py:17
  63.2 4.5 reduce-window.14
  68.3 5.8 %fusion.9 = pred[1536]{0:T(1024)(128)(4,1)S(1)} fusion(pred[1536]{0:T(1024)(128)(4,1)} %constant.173, pred[1536]{0:T(1024)(128)(4,1)} %constant.174, pred[1536]{0:T(1024)(128)(4,1)} %constant.175, pred[1536]{0:T(1024)(128)(4,1)} %constant.176, pred[1536]{0:T(1024)(128)(4,1)} %constant.177, pred[1536]{0:T(1024)(128)(4,1)} %constant.178, ...), kind=kLoop, calls=%fused_computation.40 | loop fusion | flops 21504 | bytes 12320 | tf_op jit(solution)/shard_map/lt | solution.py:17
  74.3 5.8 %select_select_fusion = s32[1536]{0:T(1024)S(1)} fusion(pred[1536]{0:T(1024)(128)(4,1)} %constant.173, pred[1536]{0:T(1024)(128)(4,1)} %constant.174, pred[1536]{0:T(1024)(128)(4,1)} %constant.175, pred[1536]{0:T(1024)(128)(4,1)} %constant.176, pred[1536]{0:T(1024)(128)(4,1)} %constant.177, pred[1536]{0:T(1024)(128)(4,1)} %constant.178, ...), kind=kLoop, calls=%fused_computation.44 | loop fusion | flops 10752 | bytes 16928 | tf_op jit(solution)/shard_map/jit(_take)/gather | solution.py:16
  80.1 6.2 %scatter_custom_fusion = s32[3072]{0:T(1024)S(1)} fusion(s32[1536]{0:T(1024)S(1)} %fusion.17, s32[1536]{0:T(1024)S(1)} %broadcast.267, s32[]{:T(128)} %constant.149.clone.1), kind=kCustom, calls=%fused_computation.58 | custom fusion | bytes 12292 | tf_op jit(solution)/shard_map/scatter | solution.py:26
  86.3 6.4 %scatter_custom_fusion.1 = s32[3072]{0:T(1024)S(1)} fusion(s32[1536]{0:T(1024)S(1)} %fusion.17, s32[1536]{0:T(1024)S(1)} %iota.38, s32[]{:T(128)} %constant.149.clone.1), kind=kCustom, calls=%fused_computation.55 | custom fusion | bytes 12292 | tf_op jit(solution)/shard_map/scatter | solution.py:25
  92.7 10.5 %gather_fusion = bf16[1536,1024]{1,0:T(8,128)(2,1)} fusion(bf16[2000,1024]{1,0:T(8,128)(2,1)} %param.16, s32[2048]{0:T(1024)S(1)} %pad_clamp_fusion), kind=kCustom, calls=%fused_computation | custom fusion | bytes 6297600 | tf_op jit(solution)/shard_map/gather | solution.py:65
  103.2 3.5 broadcast_select_fusion.3
  106.7 18.1 %gather_fusion.1 = bf16[3072,1024]{1,0:T(8,128)(2,1)} fusion(bf16[1536,1024]{1,0:T(8,128)(2,1)} %broadcast_select_fusion.3, s32[3072]{0:T(1024)S(1)} %fusion.8), kind=kCustom, calls=%fused_computation.1 | custom fusion | bytes 12595200 | tf_op jit(solution)/shard_map/gather | solution.py:73
  124.9 7.6 %convert_select_fusion = f32[3072,1,1024]{2,0,1:T(8,128)} fusion(bf16[3072,1024]{1,0:T(8,128)(2,1)} %gather_fusion.1, pred[3072]{0:T(1024)(128)(4,1)S(1)} %broadcast_compare_fusion), kind=kLoop, calls=%fused_computation.6 | loop fusion | flops 6291456 | bytes 18877440 | tf_op jit(solution)/shard_map/jit(_where)/select_n | solution.py:73
  132.5 6.6 %copy.16 = bf16[1536,3,512]{0,2,1:T(8,128)(2,1)} copy(bf16[1536,3,512]{2,0,1:T(8,128)(2,1)} %all-gather.3.cloned.1.call-done) | data formatting | bytes 9437184 | tf_op jit(solution)/shard_map/all_gather | solution.py:48
  139.1 6.6 %copy.17 = bf16[1536,1536]{1,0:T(8,128)(2,1)} copy(bf16[1536,1536]{0,1:T(8,128)(2,1)} %bitcast.58) | data formatting | bytes 9437184 | tf_op jit(solution)/shard_map/reshape | solution.py:58
  145.7 22.3 %gather_fusion.2 = bf16[3072,1536]{1,0:T(8,128)(2,1)} fusion(bf16[1536,1536]{1,0:T(8,128)(2,1)} %copy.17, s32[3072]{0:T(1024)S(1)} %fusion.8), kind=kCustom, calls=%fused_computation.2 | custom fusion | bytes 18886656 | tf_op jit(solution)/shard_map/gather | solution.py:71
  167.9 13.3 %convolution_bitcast_fusion = f32[3072,1,1024]{2,0,1:T(8,128)S(1)} fusion(bf16[1536,1024]{1,0:T(8,128)(2,1)S(1)} %bitcast.57, bf16[3072,1536]{1,0:T(8,128)(2,1)} %gather_fusion.2, pred[3072]{0:T(1024)(128)(4,1)S(1)} %broadcast_compare_fusion), kind=kOutput, calls=%fused_computation.8 | convolution fusion | flops 9668395008 | bytes 25168896 | tf_op jit(solution)/shard_map/dot_general | solution.py:72
  181.2 14.2 %pad_maximum_fusion = f32[3072,2,1024]{2,0,1:T(8,128)} fusion(f32[3072,1,1024]{2,0,1:T(8,128)S(1)} %convolution_bitcast_fusion, f32[3072,1,1024]{2,0,1:T(8,128)} %convert_select_fusion), kind=kLoop, calls=%fused_computation.5 | loop fusion | flops 6291456 | bytes 50331648 | tf_op jit(solution)/shard_map/stack | solution.py:75
  195.6 255.0 %reduce-scatter.2.cloned.1.call-done = f32[192,2,1024]{2,0,1:T(8,128)} async-done(((f32[3072,2,1024]{2,0,1:T(8,128)}), f32[192,2,1024]{2,0,1:T(8,128)}) %reduce-scatter.2.cloned.1.call-update) | async-done | bytes 1572880 | tf_op jit(solution)/shard_map/reduce_scatter | solution.py:74
  450.6 1.3 fusion.1
  451.9 1.3 multiply_reduce_fusion.1
  453.2 24.0 %psum.14 = f32[192,2]{0,1:T(2,128)S(1)} all-reduce(f32[192,2]{0,1:T(2,128)S(1)} %pad_maximum_fusion.2), channel_id=1, replica_groups=mesh['replica'=8,'tensor'=16] {'replica'}, use_global_device_ids=true, to_apply=%region_8.9 | all-reduce | flops 384 | bytes 3072 | tf_op jit(solution)/shard_map/psum | solution.py:83
  477.2 1.4 multiply_reduce_fusion
  478.7 19.2 %psum.15 = f32[192]{0:T(256)S(1)} all-reduce(f32[192]{0:T(256)S(1)} %multiply_reduce_fusion), channel_id=1, replica_groups=mesh['replica'=8,'tensor'=16] {'replica'}, use_global_device_ids=true, to_apply=%region_10.11 | all-reduce | flops 192 | bytes 1536 | tf_op jit(solution)/shard_map/psum | solution.py:87
  497.9 2.1 multiply_convert_fusion
  500.0 1.6 multiply_convert_fusion.2
  501.7 1.7 copy.18
  503.4 43.5 %all-gather.5.cloned.1.call-done = bf16[3072,1024]{1,0:T(8,128)(2,1)} async-done(((bf16[192,1024]{1,0:T(8,128)(2,1)}), bf16[3072,1024]{1,0:T(8,128)(2,1)}) %all-gather.5.cloned.1.call-update) | async-done | bytes 6291472 | tf_op jit(solution)/shard_map/all_gather | solution.py:93
  546.9 16.5 %fusion = f32[1536,1024]{1,0:T(8,128)} fusion(bf16[3072,1024]{1,0:T(8,128)(2,1)} %all-gather.5.cloned.1.call-done, bf16[3072,1536]{1,0:T(8,128)(2,1)} %gather_fusion.2, pred[3072]{0:T(1024)(128)(4,1)S(1)} %broadcast_compare_fusion), kind=kOutput, calls=%fused_computation.9 | convolution fusion | flops 9668395008 | bytes 22023168 | tf_op jit(solution)/shard_map/dot_general | solution.py:98
  (37 shorter events, 1.9 us)
Async XLA Ops:
  7.2 160.8 %copy-start = (bf16[3,512,1024]{2,1,0:T(8,128)(2,1)S(1)}, bf16[3,512,1024]{2,1,0:T(8,128)(2,1)}, u32[]{:S(2)}) copy-start(bf16[3,512,1024]{2,1,0:T(8,128)(2,1)} %param.15) | copy-start | bytes 9437188
  7.2 125.3 %all-gather.3.cloned.1.call-start = ((), (), s32[]{:S(2)}) async-start(), calls=%async_computation.1 | async-start | bytes 5308416 | tf_op jit(solution)/shard_map/all_gather | solution.py:48
  7.9 442.7 %reduce-scatter.2.cloned.1.call-start = ((), (), s32[]{:S(2)}) async-start(), calls=%async_computation.2 | async-start | bytes 26738688 | tf_op jit(solution)/shard_map/reduce_scatter | solution.py:74
  195.5 281.7 %copy-start.2 = (bf16[192,1024]{1,0:T(8,128)(2,1)S(1)}, bf16[192,1024]{1,0:T(8,128)(2,1)}, u32[]{:S(2)}) copy-start(bf16[192,1024]{1,0:T(8,128)(2,1)} %param.19) | copy-start | bytes 1179652
  195.5 281.8 %copy-start.3 = (f32[1024]{0:T(1024)S(1)}, f32[1024]{0:T(1024)}, u32[]{:S(2)}) copy-start(f32[1024]{0:T(1024)} %param.18) | copy-start | bytes 12292
  195.5 304.6 %copy-start.4 = (f32[1024]{0:T(1024)S(1)}, f32[1024]{0:T(1024)}, u32[]{:S(2)}) copy-start(f32[1024]{0:T(1024)} %param.17) | copy-start | bytes 12292
  195.5 351.4 %all-gather.5.cloned.1.call-start = ((), (), s32[]{:S(2)}) async-start(), calls=%async_computation.3 | async-start | bytes 6684672 | tf_op jit(solution)/shard_map/all_gather | solution.py:93
  546.9 16.5 %copy-start.1 = (bf16[3,512,1024]{2,1,0:T(8,128)(2,1)S(1)}, bf16[3,512,1024]{2,1,0:T(8,128)(2,1)}, u32[]{:S(2)}) copy-start(bf16[3,512,1024]{2,1,0:T(8,128)(2,1)} %param.15) | copy-start | bytes 9437188
Sparse Core Ops, SparseCore 0:
  10.3 78.7 all-gather.2
  195.6 254.9 reduce-scatter.1
  500.2 46.6 all-gather.4
where the time goes:
time: 572 us; the launch traced here: 570 us
  waiting for transfers between devices  299 us (52%)
  blocking collectives  86.8 us (15%)
  local copies, waits for them, and re-layouts  83.2 us (15%)
  other arithmetic  55.4 us (10%)
  matrix products  29.7 us (5%)
  between operations  15.4 us (3%)
    reduce_scatter x1, waiting for transfers between devices, body(): lax.psum_scatter(jnp.stack([looked, product], axis=1), 'tensor', scatter_...  255 us
    unnamed x1, blocking collectives  43.5 us
    all_gather x1, waiting for transfers between devices, body(): shard_rows = lax.all_gather(united_grad, 'tensor', axis=0, tiled=True)  43.5 us
    psum x1, blocking collectives, body(): total_squares = lax.psum(squares, 'replica')  24 us
    gather x1, local copies, waits for them, and re-layouts, body(): chosen = jnp.where(present, row_feats[picked], jnp.zeros((), jnp.bfloat16))  22.3 us
    psum x1, blocking collectives, body(): normed_inner = lax.psum(jnp.sum(normed * weighted, axis=1), 'replica')  19.2 us
    gather x1, local copies, waits for them, and re-layouts, body(): embed_rows[picked].astype(jnp.float32)  18.1 us
    dot_general x1, matrix products, body(): lax.dot_general(chosen, shard_rows, (((0,), (0,)), ((), ())), preferred_e...  16.5 us
  transfers between devices with their start and end apart: 3, of which 2 were waited for; matrix products, arithmetic and copies ran while one was open for 15% of the time, Pallas kernels for 0%

commit v1 on v0

v1 whole, which is shorter than its diff:
```python
import functools

import jax
import jax.numpy as jnp
from jax import lax
from jax.experimental import pallas as pl
from jax.experimental.pallas import tpu as pltpu
from jax.sharding import PartitionSpec as P

TAPS = 3
EPSILON = 1e-05
BF = jnp.bfloat16
F32 = jnp.float32
I32 = jnp.int32
SPREAD = 112
CHUNK = 48
RIDE = 32
LONG = pl.CostEstimate(flops=10**11, bytes_accessed=10**9, transcendentals=0)
SHORT = pl.CostEstimate(flops=10**6, bytes_accessed=10**5, transcendentals=0)
MIB = 1024 * 1024
OWNERS = 16
REPLICAS = 8

CHIP_GROUPS = [[2 * chip + core for chip in range(8)] for core in (0, 1)]
CORE_SWAP = [(i, i ^ 1) for i in range(16)]
Y_SWAP = [(i, i ^ 4) for i in range(8)]
Z_UP = [(i, i // 4 * 4 + (i + 1) % 4) for i in range(8)]
Z_DOWN = [(i, i // 4 * 4 + (i + 3) % 4) for i in range(8)]


def to_chips(x):
    return lax.all_to_all(x, "tensor", 0, 0, axis_index_groups=CHIP_GROUPS)


def from_replicas(x):
    spread = jnp.broadcast_to(x[None], (REPLICAS,) + x.shape)
    return lax.all_to_all(spread, "replica", 0, 0)


def swap_cores(x):
    return lax.ppermute(x, "tensor", CORE_SWAP)


def dot(a, b):
    return jnp.dot(a, b, preferred_element_type=F32)


def together(*xs):
    return lax.optimization_barrier(xs)


def pick(x, index, axis=0):
    return lax.dynamic_index_in_dim(x, index, axis, keepdims=False)


def whole(shape):
    return pl.BlockSpec(shape, lambda *_: (0,) * len(shape))


def project(sides, weight, which, out_dtype, cost):
    per_server, cols = sides[0][0].shape[1], weight.shape[1]
    first = len(sides[0])
    total = first + len(sides[1])

    def kernel(which_ref, *refs):
        w_ref, out_ref = refs[total:]

        def run(pieces):
            x = jnp.concatenate(
                [jnp.concatenate([p[t] for p in pieces], axis=0) for t in range(TAPS)], axis=1
            )
            out_ref[...] = dot(x, w_ref[...]).astype(out_ref.dtype)

        @pl.when(which_ref[0] == 0)
        def _():
            run(refs[:first])

        @pl.when(which_ref[0] != 0)
        def _():
            run(refs[first:total])

    vmem = pl.BlockSpec()
    return pl.pallas_call(
        kernel,
        out_shape=jax.ShapeDtypeStruct((2 * per_server, cols), out_dtype),
        in_specs=[pl.BlockSpec(memory_space=pltpu.SMEM)] + [vmem] * (total + 1),
        out_specs=vmem,
        compiler_params=pltpu.CompilerParams(vmem_limit_bytes=24 * 1024 * 1024),
        cost_estimate=cost,
        name="project",
    )(which.reshape(1), *sides[0], *sides[1], weight)


def sum_and_spread(parts, extra):
    chips, each, cols = parts.shape
    more = extra.shape[1]

    def kernel(parts_ref, extra_ref, out_ref):
        out_ref[:, each : each + more] = extra_ref[...]
        for first in range(0, each, 16):
            here = slice(first, first + 16)
            total = parts_ref[0, here].astype(F32)
            for k in range(1, chips):
                total = total + parts_ref[k, here].astype(F32)
            total = total.astype(BF)
            for k in range(chips):
                out_ref[k, here] = total

    vmem = pl.BlockSpec()
    return pl.pallas_call(
        kernel,
        out_shape=jax.ShapeDtypeStruct((chips, each + more, cols), BF),
        in_specs=[vmem] * 2,
        out_specs=vmem,
        compiler_params=pltpu.CompilerParams(vmem_limit_bytes=16 * MIB),
        cost_estimate=SHORT,
        name="sum_and_spread",
    )(parts, extra)


def take_rows(position, value, tables, count, step):
    length, cols = tables[0].shape
    total = position.shape[1]

    def kernel(position_ref, value_ref, *refs):
        first = pl.program_id(0) * step
        row = lax.broadcasted_iota(I32, (step, total), 0) + first
        match = row == position_ref[...]
        index = jnp.sum(jnp.where(match, value_ref[...] + 1, 0), axis=1, keepdims=True) - 1
        found = None
        for at, table_ref in enumerate(refs[:-1]):
            hot = lax.broadcasted_iota(I32, (step, length), 1) + at * length == index
            part = dot(jnp.where(hot, 1.0, 0.0).astype(BF), table_ref[...])
            found = part if found is None else found + part
        refs[-1][...] = found.astype(BF)

    return pl.pallas_call(
        kernel,
        grid=(count // step,),
        out_shape=jax.ShapeDtypeStruct((count, cols), BF),
        in_specs=[whole((1, total)), whole((1, total))] + [whole((length, cols))] * len(tables),
        out_specs=pl.BlockSpec((step, cols), lambda i: (i, 0)),
        compiler_params=pltpu.CompilerParams(vmem_limit_bytes=40 * MIB),
        cost_estimate=LONG,
        name="take_rows",
    )(position, value, *tables)


def add_halves(keeps, received):
    pair, cols = keeps[0].shape
    each = pair // 8

    def kernel(k0, r0, k1, r1, out_ref):
        for chip in range(8):
            rows = slice(chip * each, chip * each + each)
            for at, (k, r) in enumerate(((k0, r0), (k1, r1))):
                total = (k[rows] + r[rows].astype(F32)).astype(BF)
                out_ref[chip, at * each : at * each + each] = total

    vmem = pl.BlockSpec()
    return pl.pallas_call(
        kernel,
        out_shape=jax.ShapeDtypeStruct((8, 2 * each, cols), BF),
        in_specs=[vmem] * 4,
        out_specs=vmem,
        compiler_params=pltpu.CompilerParams(vmem_limit_bytes=16 * MIB),
        cost_estimate=SHORT,
        name="add_halves",
    )(keeps[0], received[0], keeps[1], received[1])


def add_split(a, b, parts):
    size = a.shape[0] // parts
    cols = a.shape[1]

    def kernel(a_ref, b_ref, *outs):
        for k, out in enumerate(outs):
            out[...] = a_ref[k * size : k * size + size] + b_ref[k * size : k * size + size]

    vmem = pl.BlockSpec()
    return pl.pallas_call(
        kernel,
        out_shape=[jax.ShapeDtypeStruct((size, cols), BF)] * parts,
        in_specs=[vmem] * 2,
        out_specs=[vmem] * parts,
        compiler_params=pltpu.CompilerParams(vmem_limit_bytes=16 * MIB),
        cost_estimate=SHORT,
        name="add_split",
    )(a, b)


def rows_at(united_refs, place):
    ref = united_refs[place // 4]
    size = CHUNK
    chunk = place % 4 // 2
    block = ref[4 * (place % 2) : 4 * (place % 2) + 4, chunk * size : chunk * size + size]
    return block.reshape(4 * size, ref.shape[2])


def landed_rows(own_ref):
    block = own_ref[:, 2 * CHUNK : 2 * CHUNK + RIDE].astype(F32)[:, :24]
    return block.reshape(8 * 24, block.shape[2])


def column_of(row, size):
    eye = lax.broadcasted_iota(I32, (size, size), 0) == lax.broadcasted_iota(I32, (size, size), 1)
    return jnp.sum(jnp.where(eye, row, 0.0), axis=1, keepdims=True)


def row_of(column, size):
    eye = lax.broadcasted_iota(I32, (size, size), 0) == lax.broadcasted_iota(I32, (size, size), 1)
    return jnp.sum(jnp.where(eye, column, 0.0), axis=0, keepdims=True)


def half_sums(rows, cots, gain, per_server):
    cols = gain.shape[1]
    side = 4 * per_server

    def kernel(rows_ref, cots_ref, gain_ref, out_ref):
        for k in range(4):
            u = rows_at((rows_ref,), k).astype(F32)
            w = cots_ref[k * per_server : k * per_server + per_server].astype(F32) * gain_ref[...]
            square = row_of(jnp.sum(u * u, axis=1, keepdims=True), per_server)
            inner = row_of(jnp.sum(u * w, axis=1, keepdims=True), per_server)
            out_ref[k] = jnp.concatenate([square, inner], axis=0)

    return pl.pallas_call(
        kernel,
        grid=(1,),
        out_shape=jax.ShapeDtypeStruct((4, 2, per_server), F32),
        in_specs=[
            whole(rows.shape),
            pl.BlockSpec((side, cols), lambda i: (0, 0)),
            whole((1, cols)),
        ],
        out_specs=whole((4, 2, per_server)),
        compiler_params=pltpu.CompilerParams(vmem_limit_bytes=24 * MIB),
        cost_estimate=SHORT,
        name="half_sums",
    )(rows, cots, gain)


def partial_sums(order, sums, own, other, cots, gain, per_server):
    cols = gain.shape[1]
    side = 4 * per_server

    def kernel(order_ref, sums_ref, own_ref, other_ref, cots_ref, gain_ref, out_ref):
        for k in range(4):
            u = rows_at((other_ref,), k).astype(F32)
            w = cots_ref[k * per_server : k * per_server + per_server].astype(F32) * gain_ref[...]
            square = row_of(jnp.sum(u * u, axis=1, keepdims=True), per_server)
            inner = row_of(jnp.sum(u * w, axis=1, keepdims=True), per_server)
            both = jnp.concatenate([square, inner], axis=0)
            for to in range(REPLICAS):
                out_ref[to, order_ref[k]] = sums_ref[k]
                out_ref[to, order_ref[k + 4]] = both
        e = landed_rows(own_ref).astype(F32)
        square = row_of(jnp.sum(e * e, axis=1, keepdims=True), per_server)
        both = jnp.concatenate([square, square], axis=0)
        for to in range(REPLICAS):
            out_ref[to, REPLICAS] = both

    shape = (REPLICAS, REPLICAS + 1, 2, per_server)
    return pl.pallas_call(
        kernel,
        grid=(1,),
        out_shape=jax.ShapeDtypeStruct(shape, F32),
        in_specs=[
            pl.BlockSpec(memory_space=pltpu.SMEM),
            whole(sums.shape),
            whole(own.shape),
            whole(other.shape),
            pl.BlockSpec((side, cols), lambda i: (1, 0)),
            whole((1, cols)),
        ],
        out_specs=whole(shape),
        compiler_params=pltpu.CompilerParams(vmem_limit_bytes=24 * MIB),
        cost_estimate=SHORT,
        name="partial_sums",
    )(order, sums, own, other, cots, gain)


def turn(pieces):
    taps, _, feat = pieces[0].shape
    rows = sum(piece.shape[1] for piece in pieces)

    def kernel(*refs):
        x = jnp.concatenate([ref[0] for ref in refs[:-1]], axis=0)
        refs[-1][0] = x.T

    return pl.pallas_call(
        kernel,
        grid=(taps,),
        out_shape=jax.ShapeDtypeStruct((taps, feat, rows), BF),
        in_specs=[pl.BlockSpec((1, p.shape[1], feat), lambda t: (t, 0, 0)) for p in pieces],
        out_specs=pl.BlockSpec((1, feat, rows), lambda t: (t, 0, 0)),
        compiler_params=pltpu.CompilerParams(vmem_limit_bytes=24 * MIB),
        cost_estimate=SHORT,
        name="turn",
    )(*pieces)


def weight_gradient(order, core, turned, united, cots, gain, totals, model):
    taps, feat, rows = turned.shape
    per_server = rows // REPLICAS
    cols = cots.shape[1]
    places = ([0, 1, 4, 5, 2, 3, 6, 7], [4, 5, 0, 1, 6, 7, 2, 3])

    def kernel(order_ref, core_ref, *refs):
        united_refs = refs[1:3]
        turned_ref, cots_ref, gain_ref, totals_ref, out_ref, g_ref = refs[:1] + refs[3:]

        @pl.when(pl.program_id(0) == 0)
        def _():
            for place in range(REPLICAS):
                both = totals_ref[0, order_ref[place]]
                for source in range(1, REPLICAS):
                    both = both + totals_ref[source, order_ref[place]]
                r = lax.rsqrt(both[0:1] / model + EPSILON)
                s = r * r * both[1:2] / model
                r = column_of(r, per_server)
                s = column_of(s, per_server)
                here = jnp.where(core_ref[0] == 0, places[0].index(place), places[1].index(place))
                size = per_server // 4
                for part in range(4):
                    at = part * size
                    chunk = place % 4 // 2 * size
                    u = united_refs[place // 4][4 * (place % 2) + part, chunk : chunk + size]
                    u = u.astype(F32)
                    w = cots_ref[place * per_server + at : place * per_server + at + size]
                    w = w.astype(F32) * gain_ref[...]
                    g = r[at : at + size] * (w - u * s[at : at + size])
                    start = pl.multiple_of(here * per_server + at, size)
                    g_ref[pl.ds(start, size)] = g.astype(BF)

        out_ref[0] = dot(turned_ref[0], g_ref[...])

    smem = pl.BlockSpec(memory_space=pltpu.SMEM)
    return pl.pallas_call(
        kernel,
        grid=(taps,),
        out_shape=jax.ShapeDtypeStruct((taps, feat, cols), F32),
        in_specs=[smem, smem]
        + [pl.BlockSpec((1, feat, rows), lambda t: (t, 0, 0))]
        + [whole(united[0].shape)] * 2
        + [whole((rows, cols)), whole((1, cols)), whole(totals.shape)],
        out_specs=pl.BlockSpec((1, feat, cols), lambda t: (t, 0, 0)),
        scratch_shapes=[pltpu.VMEM((rows, cols), BF)],
        compiler_params=pltpu.CompilerParams(vmem_limit_bytes=48 * MIB),
        cost_estimate=LONG,
        name="weight_gradient",
    )(order, core.reshape(1), turned, *united, cots, gain, totals)


def slot_rows(order, position, united, capacity):
    cols = united[0].shape[2]
    per_server = position.shape[2]

    def kernel(order_ref, position_ref, own_ref, other_ref, out_ref):
        slot = lax.broadcasted_iota(I32, (capacity, per_server), 0)
        found = jnp.zeros((capacity, cols), F32)
        for place in range(REPLICAS):
            match = slot == position_ref[order_ref[place]]
            hot = jnp.where(match, 1.0, 0.0).astype(BF)
            found = found + dot(hot, rows_at((own_ref, other_ref), place))
        out_ref[...] = found.astype(BF)

    vmem = pl.BlockSpec()
    return pl.pallas_call(
        kernel,
        out_shape=jax.ShapeDtypeStruct((capacity, cols), BF),
        in_specs=[pl.BlockSpec(memory_space=pltpu.SMEM)] + [vmem] * 3,
        out_specs=vmem,
        compiler_params=pltpu.CompilerParams(vmem_limit_bytes=24 * MIB),
        cost_estimate=SHORT,
        name="slot_rows",
    )(order, position, *united)


def normed_rows(position, found, own, gain, embed_gain, totals, model):
    capacity, cols = found.shape
    per_server = position.shape[2]

    def kernel(
        position_ref, found_ref, own_ref, gain_ref, embed_gain_ref, totals_ref, embed_ref, out_ref
    ):
        slot = lax.broadcasted_iota(I32, (capacity, per_server), 0)
        r_slot = jnp.zeros((capacity, 1), F32)
        for replica in range(REPLICAS + 1):
            square = totals_ref[0, replica]
            for source in range(1, REPLICAS):
                square = square + totals_ref[source, replica]
            r = lax.rsqrt(square[0:1] / model + EPSILON)
            if replica < REPLICAS:
                match = slot == position_ref[replica]
                r_slot = r_slot + jnp.sum(jnp.where(match, r, 0.0), axis=1, keepdims=True)
            else:
                r_embed = column_of(r, per_server)
        out_ref[...] = (found_ref[...].astype(F32) * r_slot * gain_ref[...]).astype(BF)
        embed_ref[...] = (landed_rows(own_ref) * r_embed * embed_gain_ref[...]).astype(BF)

    vmem = pl.BlockSpec()
    return pl.pallas_call(
        kernel,
        out_shape=[jax.ShapeDtypeStruct((capacity, cols), BF)] * 2,
        in_specs=[vmem] * 6,
        out_specs=[vmem] * 2,
        compiler_params=pltpu.CompilerParams(vmem_limit_bytes=16 * MIB),
        cost_estimate=SHORT,
        name="normed_rows",
    )(position, found, own, gain, embed_gain, totals)


def body(
    features,
    accepted,
    owner,
    draft_ids,
    fc_weight,
    embed_table,
    embed_gain,
    hidden_gain,
    hidden_grad,
):
    tensor_index = lax.axis_index("tensor")
    replica_index = lax.axis_index("replica")
    core = tensor_index % 2
    y_hi = replica_index // 4
    z = replica_index % 4
    per_server = features.shape[0]
    capacity = hidden_grad.shape[0]
    steps = capacity // OWNERS
    feat = features.shape[2]
    width = TAPS * feat
    cols = fc_weight.shape[2]
    model = cols * REPLICAS
    rows = per_server * REPLICAS
    pair = 2 * per_server

    weight = fc_weight.reshape(width, cols)

    with jax.named_scope("gather_cotangents"):
        grads = lax.all_gather(hidden_grad, "tensor", axis=0, tiled=True)

    with jax.named_scope("row_codes"):
        accepted_here = jnp.arange(per_server, dtype=I32) < accepted[0]
        code = jnp.where(accepted_here, owner[:, 0], OWNERS) * 32768 + draft_ids
        code = jnp.broadcast_to(code.reshape(1, 1, per_server), (REPLICAS, 1, per_server))
        codes = lax.all_to_all(code, "replica", 0, 0)

    with jax.named_scope("gather_features"):
        mine = features.transpose(1, 0, 2)
        before_z = lax.ppermute(mine, "replica", Z_UP)
        after_z = lax.ppermute(mine, "replica", Z_DOWN)
        across = lax.ppermute(mine, "replica", Y_SWAP)
    mine, before_z, after_z, across, codes = together(mine, before_z, after_z, across, codes)
    pieces_first = ((mine, before_z), (after_z, across))

    with jax.named_scope("gather_features"):
        across_before = lax.ppermute(across, "replica", Z_UP)
        across_after = lax.ppermute(across, "replica", Z_DOWN)
        half = per_server // 2
        opposite = (
            lax.ppermute(before_z[:, :half], "replica", Z_UP),
            lax.ppermute(after_z[:, half:], "replica", Z_DOWN),
        )
    with jax.named_scope("unite_first"):
        give = project(pieces_first, weight, 1 - core, BF, LONG)
        given_first = swap_cores(give)
    with jax.named_scope("row_order"):
        up, down, two = (z + 3) % 4, (z + 1) % 4, (z + 2) % 4
        here, there = y_hi * 4, (1 - y_hi) * 4
        low = [here + z, here + up, there + up, there + down]
        high = [here + down, there + z, here + two, there + two]
        order = jnp.where(core == 0, jnp.stack(low + high), jnp.stack(high + low))
        order_hot = order[:, None] == jnp.arange(REPLICAS, dtype=I32)[None, :]
        place_of = jnp.sum(
            jnp.where(order_hot, jnp.arange(REPLICAS, dtype=I32)[:, None], 0), axis=0
        )

    with jax.named_scope("row_codes"):
        codes = codes.reshape(rows)
        row_owner = codes // 32768
        row_id = codes % 32768
        lane = jnp.arange(128, dtype=I32)
        picks = (row_owner[:, None] == lane[None, :]) & (lane[None, :] < OWNERS)
        earlier = jnp.arange(rows)[:, None] > jnp.arange(rows)[None, :]
        before = dot(earlier.astype(BF), picks.astype(BF))
        rank = jnp.sum(jnp.where(picks, before, 0.0), axis=1).astype(I32)
        counts = jnp.sum(picks.astype(I32), axis=0)[:OWNERS]
        placed = row_owner < OWNERS
        target = jnp.where(placed, row_owner * capacity + rank, -1)
        row_place = place_of[:, None] * per_server + jnp.arange(per_server, dtype=I32)[None, :]

    with jax.named_scope("embeds"):
        device_of = rank % OWNERS
        lanes = jnp.arange(OWNERS, dtype=I32)
        held = jnp.maximum(counts[:, None] - lanes[None, :] + OWNERS - 1, 0) // OWNERS
        base = jnp.cumsum(held, axis=0) - held
        row_base = jnp.sum(
            jnp.where(
                (row_owner[:, None, None] == lanes[None, :, None])
                & (device_of[:, None, None] == lanes[None, None, :]),
                base[None],
                0,
            ),
            axis=(1, 2),
        )
        vocab_local = embed_table.shape[0]
        local_id = row_id - tensor_index * vocab_local
        found = placed & (local_id >= 0) & (local_id < vocab_local)
        spot = jnp.where(found, device_of // 2 * SPREAD + row_base + rank // OWNERS, -1)
        side = device_of % 2
        give_spot = jnp.where(side != core, spot, -1).reshape(1, rows)
        keep_spot = jnp.where(side == core, spot, -1).reshape(1, rows)
        local_id = local_id.reshape(1, rows)
        embeds_give = take_rows(give_spot, local_id, (embed_table,), 8 * SPREAD, 448)
        swapped = swap_cores(embeds_give)
        keep_spot = together(keep_spot, embeds_give)[0]
        embeds_keep = take_rows(keep_spot, local_id, (embed_table,), 8 * SPREAD, 448)
        (summed_embeds,) = add_split(embeds_keep, swapped, 1)
        landed_embeds = to_chips(summed_embeds.reshape(8, SPREAD, cols))
    across_before, across_after, opposite, mine, _ = together(
        across_before, across_after, opposite, mine, summed_embeds
    )
    pieces_first = ((mine, before_z), (after_z, across))

    with jax.named_scope("gather_features"):
        across_opposite = (
            lax.ppermute(across_before[:, :half], "replica", Z_UP),
            lax.ppermute(across_after[:, half:], "replica", Z_DOWN),
        )
    with jax.named_scope("unite_first"):
        kept_first = project(pieces_first, weight, core, F32, LONG)
    across_opposite, kept_first = together(across_opposite, kept_first)
    pieces_second = ((across_before, across_after), opposite + across_opposite)

    with jax.named_scope("unite_second"):
        give = project(pieces_second, weight, 1 - core, BF, SHORT)
        given_second = swap_cores(give)
        kept_second = project(
            ((together(across_before, give)[0], across_after), pieces_second[1]),
            weight,
            core,
            F32,
            SHORT,
        )
        summed = add_halves((kept_first, kept_second), (given_first, given_second))
    summed, landed_embeds, across_opposite = together(summed, landed_embeds, across_opposite)
    pieces_second = ((across_before, across_after), opposite + across_opposite)

    gain_row = hidden_gain.reshape(1, cols)
    with jax.named_scope("unite"):
        parts = to_chips(summed)
    with jax.named_scope("embeds"):
        arrived = jnp.sum(landed_embeds.astype(F32), axis=0).astype(BF)
        my_held = pick(held, tensor_index, 1)
        my_base = pick(base, tensor_index, 1)
        step = jnp.arange(steps, dtype=I32)
        want = jnp.where(step[None, :] < my_held[:, None], my_base[:, None] + step[None, :], -1)
        want = want.reshape(8, 2, steps)
        want = jnp.stack([pick(want, 1 - core, 1), pick(want, core, 1)]).reshape(capacity)
        lay = want[:, None] == jnp.arange(SPREAD, dtype=I32)[None, :]
        laid = dot(lay.astype(BF), arrived).astype(BF).reshape(2, 8, steps, cols)
        swapped = swap_cores(laid[0])
        first = jnp.where(core == 0, laid[1], swapped)
        second = jnp.where(core == 0, swapped, laid[1])
        blank = jnp.zeros((8, RIDE - 2 * steps, cols), BF)
        pairs = jnp.concatenate([first, second, blank], axis=1)
    with jax.named_scope("grad_fc"):
        turned = turn(sum(pieces_first + pieces_second, ()))
    parts, pairs, turned = together(parts, pairs, turned)

    with jax.named_scope("unite"):
        own = to_chips(sum_and_spread(parts, pairs))
    with jax.named_scope("cotangent_rows"):
        cots = take_rows(
            row_place.reshape(1, rows), target.reshape(1, rows), (grads,), rows, 384
        )

    own, cots = together(own, cots)

    with jax.named_scope("unite_second"):
        united = (own, swap_cores(own))
    with jax.named_scope("norms"):
        sums = half_sums(own, cots, gain_row, per_server)
        message = partial_sums(order, sums, own, united[1], cots, gain_row, per_server)
    united, message, position = together(
        united, message, (target - tensor_index * capacity)
    )
    position = position.reshape(REPLICAS, 1, per_server)

    with jax.named_scope("norms"):
        totals = lax.all_to_all(message, "replica", 0, 0)
    with jax.named_scope("draft_input"):
        found = slot_rows(order, position, united, capacity)
    totals, found = together(totals, found)

    with jax.named_scope("grad_fc"):
        grad_fc = weight_gradient(
            order, core, turned, united, cots, gain_row, totals, model
        )
    with jax.named_scope("draft_input"):
        draft_embed, draft_hidden = normed_rows(
            position, found, own, gain_row, embed_gain.reshape(1, cols), totals, model
        )
        draft_embed = draft_embed.reshape(OWNERS, steps, cols).transpose(1, 0, 2)
        draft_embed = draft_embed.reshape(capacity, cols)
        draft_input = jnp.stack([draft_embed, draft_hidden], axis=1)
    return (draft_input, grad_fc)


def solution(mesh):
    return jax.shard_map(
        body,
        mesh=mesh,
        in_specs=(
            P("replica", None, "tensor"),
            P("replica"),
            P("replica", None),
            P("replica"),
            P(None, "tensor", "replica"),
            P("tensor", "replica"),
            P("replica"),
            P("replica"),
            P("tensor", "replica"),
        ),
        out_specs=(P("tensor", None, "replica"), P(None, "tensor", "replica")),
        check_vma=False,
    )
```

time: 572 us -> 197 us (0.34)
  waiting for transfers between devices: 299 us -> 41.9 us
  blocking collectives: 86.8 us -> 0 us
  Pallas kernels: 0 us -> 58.4 us
  other arithmetic: 55.4 us -> 6.54 us
  local copies, waits for them, and re-layouts: 83.2 us -> 35.3 us
  starting transfers between devices: 0.12 us -> 35.8 us
  matrix products: 29.7 us -> 2.49 us
    reduce_scatter x1 -> x0, waiting for transfers between devices: 255 us -> none  [body(): lax.psum_scatter(jnp.stack([looked, product], axis=1), 'tensor', scatter_...]
    pallas_call x0 -> x16, Pallas kernels: none -> 58.4 us  [the longest x3 21.8 us: take_rows(): pl.pallas_call(kernel, grid=(count // step,), out_shape=jax.ShapeDtypeStr...]
    gather x4 -> x0, local copies, waits for them, and re-layouts: 51.5 us -> none  [the longest x1 22.3 us: body(): chosen = jnp.where(present, row_feats[picked], jnp.zeros((), jnp.bfloat16))]
    unnamed x1 -> x0, blocking collectives: 43.5 us -> none
    all_gather x2 -> x1, waiting for transfers between devices: 43.5 us -> 0.02 us  [body(): grads = lax.all_gather(hidden_grad, 'tensor', axis=0, tiled=True)]
    psum x2 -> x0, blocking collectives: 43.3 us -> none  [the longest x1 24 us: body(): total_squares = lax.psum(squares, 'replica')]
    all_to_all x0 -> x5, waiting for transfers between devices: none -> 37.5 us  [the longest x3 24.2 us: to_chips(): return lax.all_to_all(x, 'tensor', 0, 0, axis_index_groups=CHIP_GROUPS)]
    dot_general x2, matrix products: 29.7 us -> 2.49 us  [dot(): return jnp.dot(a, b, preferred_element_type=F32)]
  transfers between devices with their start and end apart: 3 -> 20, of which waited for: 2 -> 7; matrix products, arithmetic and copies ran while one was open for 15% -> 10% of each run, Pallas kernels for 0% -> 23%
where the time goes in v1:
time: 197 us; the launch traced here: 196 us
  Pallas kernels  58.4 us (30%)
  waiting for transfers between devices  41.9 us (21%)
  starting transfers between devices  35.8 us (18%)
  local copies, waits for them, and re-layouts  35.3 us (18%)
  between operations  15.3 us (8%)
  other arithmetic  6.54 us (3%)
  matrix products  2.49 us (1%)
    unnamed x77, local copies, waits for them, and re-layouts  24.6 us
    all_to_all x3, waiting for transfers between devices, to_chips(): return lax.all_to_all(x, 'tensor', 0, 0, axis_index_groups=CHIP_GROUPS)  24.2 us
    pallas_call x3, Pallas kernels, take_rows(): pl.pallas_call(kernel, grid=(count // step,), out_shape=jax.ShapeDtypeStr...  21.8 us
    pallas_call x4, Pallas kernels, project(): pl.pallas_call(kernel, out_shape=jax.ShapeDtypeStruct((2 * per_server, co...  12.5 us
    all_to_all x3, starting transfers between devices, to_chips(): return lax.all_to_all(x, 'tensor', 0, 0, axis_index_groups=CHIP_GROUPS)  11.6 us
    pallas_call x1, Pallas kernels, weight_gradient(): pl.pallas_call(kernel, grid=(taps,), out_shape=jax.ShapeDtypeStruct((taps...  11 us
    all_to_all x1, waiting for transfers between devices, body(): codes = lax.all_to_all(code, 'replica', 0, 0)  8.28 us
    all_to_all x1, waiting for transfers between devices, body(): totals = lax.all_to_all(message, 'replica', 0, 0)  4.98 us
  transfers between devices with their start and end apart: 20, of which 7 were waited for; matrix products, arithmetic and copies ran while one was open for 10% of the time, Pallas kernels for 23%

profile of v1, /device:TPU:0, one launch (start us, length us, event | category | flops | bytes accessed | tf_op | source)
XLA Modules:
  0.0 195.8 jit_solution(10524196329070663308)
XLA Ops:
  7.2 3.4 %collective-permute-start.2 = (bf16[3,192,512]{2,1,0:T(8,128)(2,1)}, bf16[3,192,512]{2,1,0:T(8,128)(2,1)}, u32[]{:S(2)}, u32[]{:S(2)}) collective-permute-start(bf16[3,192,512]{2,1,0:T(8,128)(2,1)} %bitcast.32), channel_id=1, source_target_pairs={{0,64},{16,80},{32,96},{48,112},{64,0},{80,16},{96,32},{112,48},{1... | collective-permute-start | bytes 1769480 | tf_op jit(solution)/shard_map/gather_features/ppermute | solution.py:455
  10.6 4.0 %collective-permute-start.1 = (bf16[3,192,512]{2,1,0:T(8,128)(2,1)}, bf16[3,192,512]{2,1,0:T(8,128)(2,1)S(1)}, u32[]{:S(2)}, u32[]{:S(2)}) collective-permute-start(bf16[3,192,512]{2,1,0:T(8,128)(2,1)} %bitcast.33), channel_id=1, source_target_pairs={{0,48},{16,0},{32,16},{48,32},{64,112},{80,64},{96,80},{112,96},{1... | collective-permute-start | bytes 1769480 | tf_op jit(solution)/shard_map/gather_features/ppermute | solution.py:454
  16.6 4.5 %all-to-all-start = ((s32[8,1,192]{2,1,0:T(1,128)}), s32[8,1,192]{2,1,0:T(1,128)S(1)}, u32[]{:S(2)}, u32[]{:S(2)}) async-start(s32[8,1,192]{2,1,0:T(1,128)} %broadcast_in_dim.45), calls=%async_computation | async-start | bytes 16384 | tf_op jit(solution)/shard_map/row_codes/all_to_all | solution.py:449
  22.4 8.3 %all-to-all-done = s32[8,1,192]{2,1,0:T(1,128)S(1)} async-done(((s32[8,1,192]{2,1,0:T(1,128)}), s32[8,1,192]{2,1,0:T(1,128)S(1)}, u32[]{:S(2)}, u32[]{:S(2)}) %all-to-all-start) | async-done | bytes 6176 | tf_op jit(solution)/shard_map/row_codes/all_to_all | solution.py:449
  32.8 1.7 collective-permute-start.3
  39.5 2.2 %copy-done.29 = bf16[2000,1024]{1,0:T(8,128)(2,1)S(1)} copy-done((bf16[2000,1024]{1,0:T(8,128)(2,1)S(1)}, bf16[2000,1024]{1,0:T(8,128)(2,1)}, u32[]{:S(2)}) %copy-start.29) | copy-done | bytes 4096024
  41.7 5.6 %take_rows.3 = bf16[896,1024]{1,0:T(8,128)(2,1)} custom-call(s32[1,1536]{1,0:T(1,128)S(1)} %get-tuple-element.77.position_ref, s32[1,1536]{1,0:T(1,128)S(1)} %get-tuple-element.79.value_ref, bf16[2000,1024]{1,0:T(8,128)(2,1)S(1)} %copy-done.29), custom_call_target="tpu_custom_call" | custom-call | flops 99999997952 | bytes 1000000000 | tf_op jit(solution)/shard_map/embeds/take_rows/pallas_call | solution.py:137
  47.5 4.7 %take_rows.4.a_ref = bf16[896,1024]{1,0:T(8,128)(2,1)S(1)} custom-call(s32[1,1536]{1,0:T(1,128)S(1)} %compare_select_fusion.1.position_ref, s32[1,1536]{1,0:T(1,128)S(1)} %get-tuple-element.79.value_ref, bf16[2000,1024]{1,0:T(8,128)(2,1)S(1)} %copy-done.29), custom_call_target="tpu_custom_call" | custom-call | flops 99999997952 | bytes 1000000000 | tf_op jit(solution)/shard_map/embeds/take_rows/pallas_call | solution.py:137
  52.2 3.3 %project.5 = bf16[384,1024]{1,0:T(8,128)(2,1)} custom-call(s32[1]{0:T(128)} %bitcast.5.which_ref, bf16[3,192,512]{2,1,0:T(8,128)(2,1)S(1)} %bitcast.35, bf16[3,192,512]{2,1,0:T(8,128)(2,1)S(1)} %copy-done.20, bf16[3,192,512]{2,1,0:T(8,128)(2,1)S(1)} %copy-done.16, bf16[3,192,512]{2,1,0:T(8,128)(2,1)} %collective-permute-done.2.refs_3_, ...), custom_call_target="tpu_custom_call" | custom-call | flops 99999997952 | bytes 1000000000 | tf_op jit(solution)/shard_map/unite_first/project/pallas_call | solution.py:83
  59.0 4.4 %all-to-all-start.1 = ((bf16[8,112,1024]{2,1,0:T(8,128)(2,1)}), bf16[8,112,1024]{2,1,0:T(8,128)(2,1)}, u32[]{:S(2)}, u32[]{:S(2)}) async-start(bf16[8,112,1024]{2,1,0:T(8,128)(2,1)} %bitcast.31), calls=%async_computation.1 | async-start | bytes 3670016 | tf_op jit(solution)/shard_map/embeds/all_to_all | solution.py:32
  65.4 2.8 %collective-permute-start.9 = (bf16[3,96,512]{2,1,0:T(8,128)(2,1)S(1)}, bf16[3,96,512]{2,1,0:T(8,128)(2,1)S(1)}, u32[]{:S(2)}, u32[]{:S(2)}) collective-permute-start(bf16[3,96,512]{2,1,0:T(8,128)(2,1)S(1)} %slice.28), channel_id=1, source_target_pairs={{0,48},{16,0},{32,16},{48,32},{64,112},{80,64},{96,80},{112,96},{1... | collective-permute-start | bytes 884744 | tf_op jit(solution)/shard_map/gather_features/ppermute | solution.py:531
  71.4 2.4 %project.4.k0 = f32[384,1024]{1,0:T(8,128)S(1)} custom-call(s32[1]{0:T(128)} %bitcast.3.which_ref.core_ref, bf16[3,192,512]{2,1,0:T(8,128)(2,1)S(1)} %bitcast.36, bf16[3,192,512]{2,1,0:T(8,128)(2,1)S(1)} %copy-done.21, bf16[3,192,512]{2,1,0:T(8,128)(2,1)S(1)} %copy-done.17, bf16[3,192,512]{2,1,0:T(8,128)(2,1)} %collective-permute-done.2.refs_3_, ...), custom_call_target="tpu_custom_call" | custom-call | flops 99999997952 | bytes 1000000000 | tf_op jit(solution)/shard_map/unite_first/project/pallas_call | solution.py:83
  75.0 3.0 %collective-permute-done.8.refs_4_.refs_8_ = bf16[3,96,512]{2,1,0:T(8,128)(2,1)S(1)} collective-permute-done((bf16[3,96,512]{2,1,0:T(8,128)(2,1)S(1)}, bf16[3,96,512]{2,1,0:T(8,128)(2,1)S(1)}, u32[]{:S(2)}, u32[]{:S(2)}) %collective-permute-start.8) | collective-permute-done | bytes 294944 | tf_op jit(solution)/shard_map/gather_features/ppermute | solution.py:530
  78.0 3.8 %project.6 = bf16[384,1024]{1,0:T(8,128)(2,1)} custom-call(s32[1]{0:T(128)} %bitcast.5.which_ref, bf16[3,192,512]{2,1,0:T(8,128)(2,1)} %collective-permute-done.3.refs_0_.refs_4_, bf16[3,192,512]{2,1,0:T(8,128)(2,1)} %collective-permute-done.4.refs_1_.refs_5_, bf16[3,96,512]{2,1,0:T(8,128)(2,1)} %collective-permute-done.5.refs_2_.refs_6_, ...), custom_call_target="tpu_custom_call" | custom-call | flops 1000000 | bytes 100000 | tf_op jit(solution)/shard_map/unite_second/project/pallas_call | solution.py:83
  83.5 2.9 %project.7.k1 = f32[384,1024]{1,0:T(8,128)S(1)} custom-call(s32[1]{0:T(128)} %bitcast.3.which_ref.core_ref, bf16[3,192,512]{2,1,0:T(8,128)(2,1)} %collective-permute-done.3.refs_0_.refs_4_, bf16[3,192,512]{2,1,0:T(8,128)(2,1)} %collective-permute-done.4.refs_1_.refs_5_, bf16[3,96,512]{2,1,0:T(8,128)(2,1)} %collective-permute-done.5.refs_2_.refs_6_, ...), custom_call_target="tpu_custom_call" | custom-call | flops 1000000 | bytes 100000 | tf_op jit(solution)/shard_map/unite_second/project/pallas_call | solution.py:83
  86.4 2.9 %add_halves.1 = bf16[8,96,1024]{2,1,0:T(8,128)(2,1)} custom-call(f32[384,1024]{1,0:T(8,128)S(1)} %copy-done.14, bf16[384,1024]{1,0:T(8,128)(2,1)} %collective-permute-done.10.r0, f32[384,1024]{1,0:T(8,128)S(1)} %project.7.k1, bf16[384,1024]{1,0:T(8,128)(2,1)} %collective-permute-done.11.r1), custom_call_target="tpu_custom_call" | custom-call | flops 1000000 | bytes 100000 | tf_op jit(solution)/shard_map/unite_second/add_halves/pallas_call | solution.py:161
  89.3 2.1 %all-to-all-done.1 = bf16[8,112,1024]{2,1,0:T(8,128)(2,1)} async-done(((bf16[8,112,1024]{2,1,0:T(8,128)(2,1)}), bf16[8,112,1024]{2,1,0:T(8,128)(2,1)}, u32[]{:S(2)}, u32[]{:S(2)}) %all-to-all-start.1) | async-done | bytes 1835040 | tf_op jit(solution)/shard_map/embeds/all_to_all | solution.py:32
  91.4 3.6 %all-to-all-start.2 = ((bf16[8,96,1024]{2,1,0:T(8,128)(2,1)}), bf16[8,96,1024]{2,1,0:T(8,128)(2,1)S(1)}, u32[]{:S(2)}, u32[]{:S(2)}) async-start(bf16[8,96,1024]{2,1,0:T(8,128)(2,1)} %add_halves.1), calls=%async_computation.2 | async-start | bytes 3145728 | tf_op jit(solution)/shard_map/unite/all_to_all | solution.py:32
  95.2 2.7 %reduce_sum.54 = bf16[112,1024]{1,0:T(8,128)(2,1)} reduce(bf16[8,112,1024]{2,1,0:T(8,128)(2,1)} %all-to-all-done.1, bf16[]{:T(256)} %constant.166.clone.1), dimensions={0}, to_apply=%region_4.5 | reduce | flops 802816 | bytes 2064386 | tf_op jit(solution)/shard_map/embeds/reduce_sum | solution.py:556
  104.5 3.4 %turn.1.refs_0_ = bf16[3,512,1536]{2,1,0:T(8,128)(2,1)S(1)} custom-call(bf16[3,192,512]{2,1,0:T(8,128)(2,1)S(1)} %bitcast.37, bf16[3,192,512]{2,1,0:T(8,128)(2,1)S(1)} %copy-done.22, bf16[3,192,512]{2,1,0:T(8,128)(2,1)S(1)} %copy-done.18, bf16[3,192,512]{2,1,0:T(8,128)(2,1)} %collective-permute-done.2.refs_3_, ...), custom_call_target="tpu_custom_call" | custom-call | flops 1000000 | bytes 100000 | tf_op jit(solution)/shard_map/grad_fc/turn/pallas_call | solution.py:291
  108.0 2.1 %copy-done.9 = bf16[3,512,1536]{2,1,0:T(8,128)(2,1)} copy-done((bf16[3,512,1536]{2,1,0:T(8,128)(2,1)}, bf16[3,512,1536]{2,1,0:T(8,128)(2,1)S(1)}, u32[]{:S(2)}) %copy-start.9) | copy-done | bytes 4718616
  111.3 7.9 %all-to-all-done.2.parts_ref = bf16[8,96,1024]{2,1,0:T(8,128)(2,1)S(1)} async-done(((bf16[8,96,1024]{2,1,0:T(8,128)(2,1)}), bf16[8,96,1024]{2,1,0:T(8,128)(2,1)S(1)}, u32[]{:S(2)}, u32[]{:S(2)}) %all-to-all-start.2) | async-done | bytes 1572896 | tf_op jit(solution)/shard_map/unite/all_to_all | solution.py:32
  120.7 3.6 %all-to-all-start.3 = ((bf16[8,128,1024]{2,1,0:T(8,128)(2,1)}), bf16[8,128,1024]{2,1,0:T(8,128)(2,1)S(1)}, u32[]{:S(2)}, u32[]{:S(2)}) async-start(bf16[8,128,1024]{2,1,0:T(8,128)(2,1)} %copy-done.7), calls=%async_computation.3 | async-start | bytes 4194304 | tf_op jit(solution)/shard_map/unite/all_to_all | solution.py:32
  124.4 2.8 %copy-done.28 = bf16[3072,1024]{1,0:T(8,128)(2,1)S(1)} copy-done((bf16[3072,1024]{1,0:T(8,128)(2,1)S(1)}, bf16[3072,1024]{1,0:T(8,128)(2,1)}, u32[]{:S(2)}) %copy-start.28) | copy-done | bytes 6291480
  127.1 11.4 %take_rows.5.cots_ref.refs_3_ = bf16[1536,1024]{1,0:T(8,128)(2,1)S(1)} custom-call(s32[1,1536]{1,0:T(1,128)S(1)} %add.297.position_ref, s32[1,1536]{1,0:T(1,128)S(1)} %get-tuple-element.74.value_ref, bf16[3072,1024]{1,0:T(8,128)(2,1)S(1)} %copy-done.28), custom_call_target="tpu_custom_call" | custom-call | flops 99999997952 | bytes 1000000000 | tf_op jit(solution)/shard_map/cotangent_rows/take_rows/pallas_call | solution.py:137
  138.6 1.7 copy-done.1
  140.3 14.2 %all-to-all-done.3.rows_ref.own_ref.refs_1_ = bf16[8,128,1024]{2,1,0:T(8,128)(2,1)S(1)} async-done(((bf16[8,128,1024]{2,1,0:T(8,128)(2,1)}), bf16[8,128,1024]{2,1,0:T(8,128)(2,1)S(1)}, u32[]{:S(2)}, u32[]{:S(2)}) %all-to-all-start.3) | async-done | bytes 2097184 | tf_op jit(solution)/shard_map/unite/all_to_all | solution.py:32
  154.5 1.9 copy-done.2
  158.7 2.1 %partial_sums.1 = f32[8,9,2,192]{3,2,1,0:T(2,128)} custom-call(s32[8]{0:T(128)S(1)} %broadcast_select_fusion.2.order_ref, f32[4,2,192]{2,1,0:T(2,128)S(1)} %half_sums.1.sums_ref, bf16[8,128,1024]{2,1,0:T(8,128)(2,1)S(1)} %all-to-all-done.3.rows_ref.own_ref.refs_1_, bf16[8,128,1024]{2,1,0:T(8,128)(2,1)S(1)} %collective-permute-done.13.other_ref.refs_2_, ...), custom_call_target="tpu_custom_call" | custom-call | flops 1000000 | bytes 100000 | tf_op jit(solution)/shard_map/norms/partial_sums/pallas_call | solution.py:264
  160.8 4.8 %all-to-all-start.4 = ((f32[8,9,2,192]{3,2,1,0:T(2,128)}), f32[8,9,2,192]{3,2,1,0:T(2,128)S(1)}, u32[]{:S(2)}, u32[]{:S(2)}) async-start(f32[8,9,2,192]{3,2,1,0:T(2,128)} %partial_sums.1), calls=%async_computation.4 | async-start | bytes 294912 | tf_op jit(solution)/shard_map/norms/all_to_all | solution.py:594
  168.8 5.0 %all-to-all-done.4.totals_ref.refs_5_ = f32[8,9,2,192]{3,2,1,0:T(2,128)S(1)} async-done(((f32[8,9,2,192]{3,2,1,0:T(2,128)}), f32[8,9,2,192]{3,2,1,0:T(2,128)S(1)}, u32[]{:S(2)}, u32[]{:S(2)}) %all-to-all-start.4) | async-done | bytes 110624 | tf_op jit(solution)/shard_map/norms/all_to_all | solution.py:594
  175.4 11.0 %weight_gradient.1 = f32[3,512,1024]{2,1,0:T(8,128)} custom-call(s32[8]{0:T(128)S(1)} %broadcast_select_fusion.2.order_ref, s32[1]{0:T(128)} %bitcast.3.which_ref.core_ref, bf16[3,512,1536]{2,1,0:T(8,128)(2,1)} %copy-done.9, bf16[8,128,1024]{2,1,0:T(8,128)(2,1)S(1)} %all-to-all-done.3.rows_ref.own_ref.refs_1_, bf16[8,128,1024]{2,1,0:T(8,128)(2,1)S(1)} %copy-done.6, ...), custom_call_target="tpu_custom_call" | custom-call | flops 99999997952 | bytes 1000000000 | tf_op jit(solution)/shard_map/grad_fc/weight_gradient/pallas_call | solution.py:339
  (154 shorter events, 40.2 us)
Async XLA Ops:
  7.2 117.2 %all-gather.2.cloned.1.call-start = ((), (), s32[]{:S(2)}) async-start(), calls=%async_computation.5 | async-start | bytes 6684672 | tf_op jit(solution)/shard_map/gather_cotangents/all_gather | solution.py:443
  7.2 23.5 %collective-permute-start.2 = (bf16[3,192,512]{2,1,0:T(8,128)(2,1)}, bf16[3,192,512]{2,1,0:T(8,128)(2,1)}, u32[]{:S(2)}, u32[]{:S(2)}) collective-permute-start(bf16[3,192,512]{2,1,0:T(8,128)(2,1)} %bitcast.32), channel_id=1, source_target_pairs={{0,64},{16,80},{32,96},{48,112},{64,0},{80,16},{96,32},{112,48},{1... | collective-permute-start | bytes 1769480 | tf_op jit(solution)/shard_map/gather_features/ppermute | solution.py:455
  10.6 20.1 %collective-permute-start.1 = (bf16[3,192,512]{2,1,0:T(8,128)(2,1)}, bf16[3,192,512]{2,1,0:T(8,128)(2,1)S(1)}, u32[]{:S(2)}, u32[]{:S(2)}) collective-permute-start(bf16[3,192,512]{2,1,0:T(8,128)(2,1)} %bitcast.33), channel_id=1, source_target_pairs={{0,48},{16,0},{32,16},{48,32},{64,112},{80,64},{96,80},{112,96},{1... | collective-permute-start | bytes 1769480 | tf_op jit(solution)/shard_map/gather_features/ppermute | solution.py:454
  14.6 16.1 %collective-permute-start = (bf16[3,192,512]{2,1,0:T(8,128)(2,1)}, bf16[3,192,512]{2,1,0:T(8,128)(2,1)S(1)}, u32[]{:S(2)}, u32[]{:S(2)}) collective-permute-start(bf16[3,192,512]{2,1,0:T(8,128)(2,1)} %bitcast.34), channel_id=1, source_target_pairs={{0,16},{16,32},{32,48},{48,0},{64,80},{80,96},{96,112},{112,64},{1... | collective-permute-start | bytes 1769480 | tf_op jit(solution)/shard_map/gather_features/ppermute | solution.py:453
  16.6 14.1 %all-to-all-start = ((s32[8,1,192]{2,1,0:T(1,128)}), s32[8,1,192]{2,1,0:T(1,128)S(1)}, u32[]{:S(2)}, u32[]{:S(2)}) async-start(s32[8,1,192]{2,1,0:T(1,128)} %broadcast_in_dim.45), calls=%async_computation | async-start | bytes 16384 | tf_op jit(solution)/shard_map/row_codes/all_to_all | solution.py:449
  30.7 6.0 %copy-start.15 = (bf16[3,192,512]{2,1,0:T(8,128)(2,1)}, bf16[3,192,512]{2,1,0:T(8,128)(2,1)S(1)}, u32[]{:S(2)}) copy-start(bf16[3,192,512]{2,1,0:T(8,128)(2,1)S(1)} %collective-permute-done.1.refs_2_) | copy-start | bytes 1769476
  32.4 26.6 %collective-permute-start.4 = (bf16[3,192,512]{2,1,0:T(8,128)(2,1)}, bf16[3,192,512]{2,1,0:T(8,128)(2,1)}, u32[]{:S(2)}, u32[]{:S(2)}) collective-permute-start(bf16[3,192,512]{2,1,0:T(8,128)(2,1)} %collective-permute-done.2.refs_3_), channel_id=1, source_target_pairs={{0,48},{16,0},{32,16},{48,32},{64,112},{80,64},{96,80},{112,96},{1... | collective-permute-start | bytes 1769480 | tf_op jit(solution)/shard_map/gather_features/ppermute | solution.py:461
  32.8 26.2 %collective-permute-start.3 = (bf16[3,192,512]{2,1,0:T(8,128)(2,1)}, bf16[3,192,512]{2,1,0:T(8,128)(2,1)}, u32[]{:S(2)}, u32[]{:S(2)}) collective-permute-start(bf16[3,192,512]{2,1,0:T(8,128)(2,1)} %collective-permute-done.2.refs_3_), channel_id=1, source_target_pairs={{0,16},{16,32},{32,48},{48,0},{64,80},{80,96},{96,112},{112,64},{1... | collective-permute-start | bytes 1769480 | tf_op jit(solution)/shard_map/gather_features/ppermute | solution.py:460
  35.3 12.0 %copy-start.33 = (s32[16,16]{1,0:T(8,128)}, s32[16,16]{1,0:T(8,128)S(1)}, u32[]{:S(2)}) copy-start(s32[16,16]{1,0:T(8,128)S(1)} %fusion.13) | copy-start | bytes 3076
  37.4 21.5 %collective-permute-start.6 = (bf16[3,96,512]{2,1,0:T(8,128)(2,1)}, bf16[3,96,512]{2,1,0:T(8,128)(2,1)}, u32[]{:S(2)}, u32[]{:S(2)}) collective-permute-start(bf16[3,96,512]{2,1,0:T(8,128)(2,1)} %slice.25), channel_id=1, source_target_pairs={{0,48},{16,0},{32,16},{48,32},{64,112},{80,64},{96,80},{112,96},{1... | collective-permute-start | bytes 884744 | tf_op jit(solution)/shard_map/gather_features/ppermute | solution.py:465
  38.9 20.0 %collective-permute-start.5 = (bf16[3,96,512]{2,1,0:T(8,128)(2,1)}, bf16[3,96,512]{2,1,0:T(8,128)(2,1)}, u32[]{:S(2)}, u32[]{:S(2)}) collective-permute-start(bf16[3,96,512]{2,1,0:T(8,128)(2,1)} %slice.24), channel_id=1, source_target_pairs={{0,16},{16,32},{32,48},{48,0},{64,80},{80,96},{96,112},{112,64},{1... | collective-permute-start | bytes 884744 | tf_op jit(solution)/shard_map/gather_features/ppermute | solution.py:464
  47.4 8.2 %collective-permute-start.7 = (bf16[896,1024]{1,0:T(8,128)(2,1)}, bf16[896,1024]{1,0:T(8,128)(2,1)}, u32[]{:S(2)}, u32[]{:S(2)}) collective-permute-start(bf16[896,1024]{1,0:T(8,128)(2,1)} %take_rows.3), channel_id=1, source_target_pairs={{0,1},{1,0},{2,3},{3,2},{4,5},{5,4},{6,7},{7,6},{8,9},{9,8},{10,11... | collective-permute-start | bytes 5505032 | tf_op jit(solution)/shard_map/embeds/ppermute | solution.py:41
  55.6 30.8 %collective-permute-start.10 = (bf16[384,1024]{1,0:T(8,128)(2,1)}, bf16[384,1024]{1,0:T(8,128)(2,1)}, u32[]{:S(2)}, u32[]{:S(2)}) collective-permute-start(bf16[384,1024]{1,0:T(8,128)(2,1)} %project.5), channel_id=1, source_target_pairs={{0,1},{1,0},{2,3},{3,2},{4,5},{5,4},{6,7},{7,6},{8,9},{9,8},{10,11... | collective-permute-start | bytes 2359304 | tf_op jit(solution)/shard_map/unite_first/ppermute | solution.py:41
  59.0 32.4 %all-to-all-start.1 = ((bf16[8,112,1024]{2,1,0:T(8,128)(2,1)}), bf16[8,112,1024]{2,1,0:T(8,128)(2,1)}, u32[]{:S(2)}, u32[]{:S(2)}) async-start(bf16[8,112,1024]{2,1,0:T(8,128)(2,1)} %bitcast.31), calls=%async_computation.1 | async-start | bytes 3670016 | tf_op jit(solution)/shard_map/embeds/all_to_all | solution.py:32
  65.4 9.6 %collective-permute-start.9 = (bf16[3,96,512]{2,1,0:T(8,128)(2,1)S(1)}, bf16[3,96,512]{2,1,0:T(8,128)(2,1)S(1)}, u32[]{:S(2)}, u32[]{:S(2)}) collective-permute-start(bf16[3,96,512]{2,1,0:T(8,128)(2,1)S(1)} %slice.28), channel_id=1, source_target_pairs={{0,48},{16,0},{32,16},{48,32},{64,112},{80,64},{96,80},{112,96},{1... | collective-permute-start | bytes 884744 | tf_op jit(solution)/shard_map/gather_features/ppermute | solution.py:531
  68.2 9.8 %collective-permute-start.8 = (bf16[3,96,512]{2,1,0:T(8,128)(2,1)S(1)}, bf16[3,96,512]{2,1,0:T(8,128)(2,1)S(1)}, u32[]{:S(2)}, u32[]{:S(2)}) collective-permute-start(bf16[3,96,512]{2,1,0:T(8,128)(2,1)S(1)} %slice.27), channel_id=1, source_target_pairs={{0,16},{16,32},{32,48},{48,0},{64,80},{80,96},{96,112},{112,64},{1... | collective-permute-start | bytes 884744 | tf_op jit(solution)/shard_map/gather_features/ppermute | solution.py:530
  75.0 6.8 %copy-start.36 = (s32[8]{0:T(128)S(1)}, s32[8]{0:T(128)}, u32[]{:S(2)}) copy-start(s32[8]{0:T(128)} %stack.65) | copy-start | bytes 100
  75.0 6.8 %copy-start.37 = (s32[8]{0:T(128)S(1)}, s32[8]{0:T(128)}, u32[]{:S(2)}) copy-start(s32[8]{0:T(128)} %stack.64) | copy-start | bytes 100
  75.0 6.9 %copy-start.32 = (s32[16,16]{1,0:T(8,128)S(1)}, s32[16,16]{1,0:T(8,128)}, u32[]{:S(2)}) copy-start(s32[16,16]{1,0:T(8,128)} %copy-done.31) | copy-start | bytes 3076
  75.0 6.9 %copy-start.34 = (s32[16,16]{1,0:T(8,128)S(1)}, s32[16,16]{1,0:T(8,128)}, u32[]{:S(2)}) copy-start(s32[16,16]{1,0:T(8,128)} %copy-done.33) | copy-start | bytes 3076
  81.8 4.6 %collective-permute-start.11 = (bf16[384,1024]{1,0:T(8,128)(2,1)}, bf16[384,1024]{1,0:T(8,128)(2,1)}, u32[]{:S(2)}, u32[]{:S(2)}) collective-permute-start(bf16[384,1024]{1,0:T(8,128)(2,1)} %project.6), channel_id=1, source_target_pairs={{0,1},{1,0},{2,3},{3,2},{4,5},{5,4},{6,7},{7,6},{8,9},{9,8},{10,11... | collective-permute-start | bytes 2359304 | tf_op jit(solution)/shard_map/unite_second/ppermute | solution.py:41
  91.4 27.7 %all-to-all-start.2 = ((bf16[8,96,1024]{2,1,0:T(8,128)(2,1)}), bf16[8,96,1024]{2,1,0:T(8,128)(2,1)S(1)}, u32[]{:S(2)}, u32[]{:S(2)}) async-start(bf16[8,96,1024]{2,1,0:T(8,128)(2,1)} %add_halves.1), calls=%async_computation.2 | async-start | bytes 3145728 | tf_op jit(solution)/shard_map/unite/all_to_all | solution.py:32
  95.1 8.3 %copy-start.12 = (bf16[3,96,512]{2,1,0:T(8,128)(2,1)S(1)}, bf16[3,96,512]{2,1,0:T(8,128)(2,1)}, u32[]{:S(2)}) copy-start(bf16[3,96,512]{2,1,0:T(8,128)(2,1)} %copy-done.10) | copy-start | bytes 884740
  95.1 8.3 %copy-start.18 = (bf16[3,192,512]{2,1,0:T(8,128)(2,1)S(1)}, bf16[3,192,512]{2,1,0:T(8,128)(2,1)}, u32[]{:S(2)}) copy-start(bf16[3,192,512]{2,1,0:T(8,128)(2,1)} %copy-done.15) | copy-start | bytes 1769476
  95.2 8.3 %copy-start.22 = (bf16[3,192,512]{2,1,0:T(8,128)(2,1)S(1)}, bf16[3,192,512]{2,1,0:T(8,128)(2,1)}, u32[]{:S(2)}) copy-start(bf16[3,192,512]{2,1,0:T(8,128)(2,1)} %copy-done.19) | copy-start | bytes 1769476
  101.5 8.5 %collective-permute-start.12 = (bf16[8,12,1024]{2,1,0:T(8,128)(2,1)}, bf16[8,12,1024]{2,1,0:T(8,128)(2,1)}, u32[]{:S(2)}, u32[]{:S(2)}) collective-permute-start(bf16[8,12,1024]{2,1,0:T(8,128)(2,1)} %squeeze.22), channel_id=1, source_target_pairs={{0,1},{1,0},{2,3},{3,2},{4,5},{5,4},{6,7},{7,6},{8,9},{9,8},{10,11... | collective-permute-start | bytes 589832 | tf_op jit(solution)/shard_map/embeds/ppermute | solution.py:41
  120.7 33.8 %all-to-all-start.3 = ((bf16[8,128,1024]{2,1,0:T(8,128)(2,1)}), bf16[8,128,1024]{2,1,0:T(8,128)(2,1)S(1)}, u32[]{:S(2)}, u32[]{:S(2)}) async-start(bf16[8,128,1024]{2,1,0:T(8,128)(2,1)} %copy-done.7), calls=%async_computation.3 | async-start | bytes 4194304 | tf_op jit(solution)/shard_map/unite/all_to_all | solution.py:32
  127.1 27.4 %copy-start.26 = (f32[1024]{0:T(1024)S(1)}, f32[1024]{0:T(1024)}, u32[]{:S(2)}) copy-start(f32[1024]{0:T(1024)} %param.16) | copy-start | bytes 12292
  154.5 4.2 %collective-permute-start.13 = (bf16[8,128,1024]{2,1,0:T(8,128)(2,1)S(1)}, bf16[8,128,1024]{2,1,0:T(8,128)(2,1)S(1)}, u32[]{:S(2)}, u32[]{:S(2)}) collective-permute-start(bf16[8,128,1024]{2,1,0:T(8,128)(2,1)S(1)} %all-to-all-done.3.rows_ref.own_ref.refs_1_), channel_id=1, source_target_pairs={{0,1},{1,0},{2,3},{3,2},{4,5},{5,4},{6,7},{7,6},{8,9},{9,8},{10,11... | collective-permute-start | bytes 6291464 | tf_op jit(solution)/shard_map/unite_second/ppermute | solution.py:41
  157.2 8.4 %copy-start.35 = (s32[1536]{0:T(1024)S(1)}, s32[1536]{0:T(1024)}, u32[]{:S(2)}) copy-start(s32[1536]{0:T(1024)} %get-tuple-element.57) | copy-start | bytes 18436
  160.8 13.0 %all-to-all-start.4 = ((f32[8,9,2,192]{3,2,1,0:T(2,128)}), f32[8,9,2,192]{3,2,1,0:T(2,128)S(1)}, u32[]{:S(2)}, u32[]{:S(2)}) async-start(f32[8,9,2,192]{3,2,1,0:T(2,128)} %partial_sums.1), calls=%async_computation.4 | async-start | bytes 294912 | tf_op jit(solution)/shard_map/norms/all_to_all | solution.py:594
  175.4 11.0 %copy-start.27 = (f32[1024]{0:T(1024)S(1)}, f32[1024]{0:T(1024)}, u32[]{:S(2)}) copy-start(f32[1024]{0:T(1024)} %param.15) | copy-start | bytes 12292
  (26 other events, 68.6 us)
Sparse Core Ops, SparseCore 0:
  14.8 41.7 all-gather.1

commit v2 on v1

--- a/solution.py
+++ b/solution.py
@@ -459,14 +459,7 @@
     with jax.named_scope("gather_features"):
         across_before = lax.ppermute(across, "replica", Z_UP)
         across_after = lax.ppermute(across, "replica", Z_DOWN)
-        half = per_server // 2
-        opposite = (
-            lax.ppermute(before_z[:, :half], "replica", Z_UP),
-            lax.ppermute(after_z[:, half:], "replica", Z_DOWN),
-        )
-    with jax.named_scope("unite_first"):
-        give = project(pieces_first, weight, 1 - core, BF, LONG)
-        given_first = swap_cores(give)
+        opposite = lax.ppermute(before_z, "replica", Z_UP)
     with jax.named_scope("row_order"):
         up, down, two = (z + 3) % 4, (z + 1) % 4, (z + 2) % 4
         here, there = y_hi * 4, (1 - y_hi) * 4
@@ -520,20 +513,19 @@
         embeds_keep = take_rows(keep_spot, local_id, (embed_table,), 8 * SPREAD, 448)
         (summed_embeds,) = add_split(embeds_keep, swapped, 1)
         landed_embeds = to_chips(summed_embeds.reshape(8, SPREAD, cols))
-    across_before, across_after, opposite, mine, _ = together(
-        across_before, across_after, opposite, mine, summed_embeds
+    across_before, across_after, mine, _ = together(
+        across_before, across_after, mine, summed_embeds
     )
     pieces_first = ((mine, before_z), (after_z, across))
 
     with jax.named_scope("gather_features"):
-        across_opposite = (
-            lax.ppermute(across_before[:, :half], "replica", Z_UP),
-            lax.ppermute(across_after[:, half:], "replica", Z_DOWN),
-        )
+        across_opposite = lax.ppermute(across_after, "replica", Z_DOWN)
     with jax.named_scope("unite_first"):
+        give = project(pieces_first, weight, 1 - core, BF, LONG)
+        given_first = swap_cores(give)
         kept_first = project(pieces_first, weight, core, F32, LONG)
-    across_opposite, kept_first = together(across_opposite, kept_first)
-    pieces_second = ((across_before, across_after), opposite + across_opposite)
+    across_opposite, opposite, kept_first = together(across_opposite, opposite, kept_first)
+    pieces_second = ((across_before, across_after), (opposite, across_opposite))
 
     with jax.named_scope("unite_second"):
         give = project(pieces_second, weight, 1 - core, BF, SHORT)
@@ -547,7 +539,7 @@
         )
         summed = add_halves((kept_first, kept_second), (given_first, given_second))
     summed, landed_embeds, across_opposite = together(summed, landed_embeds, across_opposite)
-    pieces_second = ((across_before, across_after), opposite + across_opposite)
+    pieces_second = ((across_before, across_after), (opposite, across_opposite))
 
     gain_row = hidden_gain.reshape(1, cols)
     with jax.named_scope("unite"):

time: 197 us -> 192 us (0.975)
  local copies, waits for them, and re-layouts: 35.3 us -> 26 us
  waiting for transfers between devices: 41.9 us -> 49 us
    all_to_all x3, waiting for transfers between devices: 24.2 us -> 30 us  [to_chips(): return lax.all_to_all(x, 'tensor', 0, 0, axis_index_groups=CHIP_GROUPS)]
    slice x4 -> x0, local copies, waits for them, and re-layouts: 3.48 us -> none  [the longest x1 0.99 us: body(): across_after[:, half:]]
    unnamed x77 -> x61, local copies, waits for them, and re-layouts: 24.6 us -> 22 us
    ppermute x4 -> x2, starting transfers between devices: 4.79 us -> 2.77 us  [the longest x1 2.69 us: body(): across_opposite = lax.ppermute(across_after, 'replica', Z_DOWN)]
  transfers between devices with their start and end apart: 20 -> 18, of which waited for: 7 -> 8; matrix products, arithmetic and copies ran while one was open for 10% -> 6% of each run, Pallas kernels for 23% -> 23%
where the time goes in v2:
time: 192 us; the launch traced here: 191 us
  Pallas kernels  57.2 us (30%)
  waiting for transfers between devices  49 us (26%)
  starting transfers between devices  36.4 us (19%)
  local copies, waits for them, and re-layouts  26 us (14%)
  between operations  15.2 us (8%)
  other arithmetic  5.82 us (3%)
    all_to_all x3, waiting for transfers between devices, to_chips(): return lax.all_to_all(x, 'tensor', 0, 0, axis_index_groups=CHIP_GROUPS)  30 us
    unnamed x61, local copies, waits for them, and re-layouts  22 us
    pallas_call x3, Pallas kernels, take_rows(): pl.pallas_call(kernel, grid=(count // step,), out_shape=jax.ShapeDtypeStr...  20.9 us
    pallas_call x4, Pallas kernels, project(): pl.pallas_call(kernel, out_shape=jax.ShapeDtypeStruct((2 * per_server, co...  13.5 us
    all_to_all x3, starting transfers between devices, to_chips(): return lax.all_to_all(x, 'tensor', 0, 0, axis_index_groups=CHIP_GROUPS)  12.4 us
    pallas_call x1, Pallas kernels, weight_gradient(): pl.pallas_call(kernel, grid=(taps,), out_shape=jax.ShapeDtypeStruct((taps...  11 us
    all_to_all x1, waiting for transfers between devices, body(): codes = lax.all_to_all(code, 'replica', 0, 0)  8.27 us
    all_to_all x1, starting transfers between devices, body(): totals = lax.all_to_all(message, 'replica', 0, 0)  6.69 us
  transfers between devices with their start and end apart: 18, of which 8 were waited for; matrix products, arithmetic and copies ran while one was open for 6% of the time, Pallas kernels for 23%

profile of v2, /device:TPU:0, one launch (start us, length us, event | category | flops | bytes accessed | tf_op | source)
XLA Modules:
  0.0 191.3 jit_solution(10900555138387592434)
XLA Ops:
  7.2 3.4 %collective-permute-start.2 = (bf16[3,192,512]{2,1,0:T(8,128)(2,1)}, bf16[3,192,512]{2,1,0:T(8,128)(2,1)}, u32[]{:S(2)}, u32[]{:S(2)}) collective-permute-start(bf16[3,192,512]{2,1,0:T(8,128)(2,1)} %bitcast.32), channel_id=1, source_target_pairs={{0,64},{16,80},{32,96},{48,112},{64,0},{80,16},{96,32},{112,48},{1... | collective-permute-start | bytes 1769480 | tf_op jit(solution)/shard_map/gather_features/ppermute | solution.py:455
  10.6 4.0 %collective-permute-start.1 = (bf16[3,192,512]{2,1,0:T(8,128)(2,1)}, bf16[3,192,512]{2,1,0:T(8,128)(2,1)S(1)}, u32[]{:S(2)}, u32[]{:S(2)}) collective-permute-start(bf16[3,192,512]{2,1,0:T(8,128)(2,1)} %bitcast.33), channel_id=1, source_target_pairs={{0,48},{16,0},{32,16},{48,32},{64,112},{80,64},{96,80},{112,96},{1... | collective-permute-start | bytes 1769480 | tf_op jit(solution)/shard_map/gather_features/ppermute | solution.py:454
  16.6 4.5 %all-to-all-start = ((s32[8,1,192]{2,1,0:T(1,128)}), s32[8,1,192]{2,1,0:T(1,128)S(1)}, u32[]{:S(2)}, u32[]{:S(2)}) async-start(s32[8,1,192]{2,1,0:T(1,128)} %broadcast_in_dim.45), calls=%async_computation | async-start | bytes 16384 | tf_op jit(solution)/shard_map/row_codes/all_to_all | solution.py:449
  22.4 8.3 %all-to-all-done = s32[8,1,192]{2,1,0:T(1,128)S(1)} async-done(((s32[8,1,192]{2,1,0:T(1,128)}), s32[8,1,192]{2,1,0:T(1,128)S(1)}, u32[]{:S(2)}, u32[]{:S(2)}) %all-to-all-start) | async-done | bytes 6176 | tf_op jit(solution)/shard_map/row_codes/all_to_all | solution.py:449
  32.8 1.8 collective-permute-start.3
  36.5 2.2 %copy-done.22 = bf16[2000,1024]{1,0:T(8,128)(2,1)S(1)} copy-done((bf16[2000,1024]{1,0:T(8,128)(2,1)S(1)}, bf16[2000,1024]{1,0:T(8,128)(2,1)}, u32[]{:S(2)}) %copy-start.22) | copy-done | bytes 4096024
  38.8 4.8 %take_rows.3 = bf16[896,1024]{1,0:T(8,128)(2,1)S(1)} custom-call(s32[1,1536]{1,0:T(1,128)S(1)} %get-tuple-element.71.position_ref, s32[1,1536]{1,0:T(1,128)S(1)} %get-tuple-element.73.value_ref, bf16[2000,1024]{1,0:T(8,128)(2,1)S(1)} %copy-done.22), custom_call_target="tpu_custom_call" | custom-call | flops 99999997952 | bytes 1000000000 | tf_op jit(solution)/shard_map/embeds/take_rows/pallas_call | solution.py:137
  43.6 4.8 %take_rows.4.a_ref = bf16[896,1024]{1,0:T(8,128)(2,1)S(1)} custom-call(s32[1,1536]{1,0:T(1,128)S(1)} %compare_select_fusion.1.position_ref, s32[1,1536]{1,0:T(1,128)S(1)} %get-tuple-element.73.value_ref, bf16[2000,1024]{1,0:T(8,128)(2,1)S(1)} %copy-done.22), custom_call_target="tpu_custom_call" | custom-call | flops 99999997952 | bytes 1000000000 | tf_op jit(solution)/shard_map/embeds/take_rows/pallas_call | solution.py:137
  50.6 4.5 %all-to-all-start.1 = ((bf16[8,112,1024]{2,1,0:T(8,128)(2,1)}), bf16[8,112,1024]{2,1,0:T(8,128)(2,1)}, u32[]{:S(2)}, u32[]{:S(2)}) async-start(bf16[8,112,1024]{2,1,0:T(8,128)(2,1)} %bitcast.31), calls=%async_computation.1 | async-start | bytes 3670016 | tf_op jit(solution)/shard_map/embeds/all_to_all | solution.py:32
  55.1 2.7 %collective-permute-start.6 = (bf16[3,192,512]{2,1,0:T(8,128)(2,1)}, bf16[3,192,512]{2,1,0:T(8,128)(2,1)}, u32[]{:S(2)}, u32[]{:S(2)}) collective-permute-start(bf16[3,192,512]{2,1,0:T(8,128)(2,1)} %collective-permute-done.4.refs_1_.refs_5_), channel_id=1, source_target_pairs={{0,48},{16,0},{32,16},{48,32},{64,112},{80,64},{96,80},{112,96},{1... | collective-permute-start | bytes 1769480 | tf_op jit(solution)/shard_map/gather_features/ppermute | solution.py:522
  59.9 3.6 %project.5 = bf16[384,1024]{1,0:T(8,128)(2,1)} custom-call(s32[1]{0:T(128)} %bitcast.5.which_ref, bf16[3,192,512]{2,1,0:T(8,128)(2,1)S(1)} %bitcast.35, bf16[3,192,512]{2,1,0:T(8,128)(2,1)} %collective-permute-done.refs_1_, bf16[3,192,512]{2,1,0:T(8,128)(2,1)S(1)} %copy-done.16, bf16[3,192,512]{2,1,0:T(8,128)(2,1)} %collective-permute-done.2.refs_3_, ...), custom_call_target="tpu_custom_call" | custom-call | flops 99999997952 | bytes 1000000000 | tf_op jit(solution)/shard_map/unite_first/project/pallas_call | solution.py:83
  63.7 2.8 %project.4.k0 = f32[384,1024]{1,0:T(8,128)S(1)} custom-call(s32[1]{0:T(128)} %bitcast.3.which_ref.core_ref, bf16[3,192,512]{2,1,0:T(8,128)(2,1)S(1)} %bitcast.36, bf16[3,192,512]{2,1,0:T(8,128)(2,1)} %collective-permute-done.refs_1_, bf16[3,192,512]{2,1,0:T(8,128)(2,1)S(1)} %copy-done.17, bf16[3,192,512]{2,1,0:T(8,128)(2,1)} %collective-permute-done.2.refs_3_, ...), custom_call_target="tpu_custom_call" | custom-call | flops 99999997952 | bytes 1000000000 | tf_op jit(solution)/shard_map/unite_first/project/pallas_call | solution.py:83
  67.8 3.5 %collective-permute-done.6.refs_3_.refs_7_ = bf16[3,192,512]{2,1,0:T(8,128)(2,1)} collective-permute-done((bf16[3,192,512]{2,1,0:T(8,128)(2,1)}, bf16[3,192,512]{2,1,0:T(8,128)(2,1)}, u32[]{:S(2)}, u32[]{:S(2)}) %collective-permute-start.6) | collective-permute-done | bytes 589856 | tf_op jit(solution)/shard_map/gather_features/ppermute | solution.py:522
  71.3 3.9 %project.6 = bf16[384,1024]{1,0:T(8,128)(2,1)} custom-call(s32[1]{0:T(128)} %bitcast.5.which_ref, bf16[3,192,512]{2,1,0:T(8,128)(2,1)} %collective-permute-done.3.refs_0_.refs_4_, bf16[3,192,512]{2,1,0:T(8,128)(2,1)} %collective-permute-done.4.refs_1_.refs_5_, bf16[3,192,512]{2,1,0:T(8,128)(2,1)} %collective-permute-done.7.refs_2_.refs_6_, ...), custom_call_target="tpu_custom_call" | custom-call | flops 1000000 | bytes 100000 | tf_op jit(solution)/shard_map/unite_second/project/pallas_call | solution.py:83
  75.9 3.1 %project.7.k1 = f32[384,1024]{1,0:T(8,128)S(1)} custom-call(s32[1]{0:T(128)} %bitcast.3.which_ref.core_ref, bf16[3,192,512]{2,1,0:T(8,128)(2,1)} %collective-permute-done.3.refs_0_.refs_4_, bf16[3,192,512]{2,1,0:T(8,128)(2,1)} %collective-permute-done.4.refs_1_.refs_5_, bf16[3,192,512]{2,1,0:T(8,128)(2,1)} %collective-permute-done.7.refs_2_.refs_6_, ...), custom_call_target="tpu_custom_call" | custom-call | flops 1000000 | bytes 100000 | tf_op jit(solution)/shard_map/unite_second/project/pallas_call | solution.py:83
  79.1 2.8 %add_halves.1 = bf16[8,96,1024]{2,1,0:T(8,128)(2,1)} custom-call(f32[384,1024]{1,0:T(8,128)S(1)} %copy-done.11, bf16[384,1024]{1,0:T(8,128)(2,1)} %collective-permute-done.8.r0, f32[384,1024]{1,0:T(8,128)S(1)} %project.7.k1, bf16[384,1024]{1,0:T(8,128)(2,1)} %collective-permute-done.9.r1), custom_call_target="tpu_custom_call" | custom-call | flops 1000000 | bytes 100000 | tf_op jit(solution)/shard_map/unite_second/add_halves/pallas_call | solution.py:161
  82.9 4.3 %all-to-all-start.2 = ((bf16[8,96,1024]{2,1,0:T(8,128)(2,1)}), bf16[8,96,1024]{2,1,0:T(8,128)(2,1)S(1)}, u32[]{:S(2)}, u32[]{:S(2)}) async-start(bf16[8,96,1024]{2,1,0:T(8,128)(2,1)} %add_halves.1), calls=%async_computation.2 | async-start | bytes 3145728 | tf_op jit(solution)/shard_map/unite/all_to_all | solution.py:32
  87.3 1.9 %reduce_sum.54 = bf16[112,1024]{1,0:T(8,128)(2,1)S(1)} reduce(bf16[8,112,1024]{2,1,0:T(8,128)(2,1)} %all-to-all-done.1, bf16[]{:T(256)} %constant.166.clone.1), dimensions={0}, to_apply=%region_4.5 | reduce | flops 802816 | bytes 2064386 | tf_op jit(solution)/shard_map/embeds/reduce_sum | solution.py:548
  90.9 3.7 %turn.1.refs_0_ = bf16[3,512,1536]{2,1,0:T(8,128)(2,1)S(1)} custom-call(bf16[3,192,512]{2,1,0:T(8,128)(2,1)S(1)} %bitcast.37, bf16[3,192,512]{2,1,0:T(8,128)(2,1)} %collective-permute-done.refs_1_, bf16[3,192,512]{2,1,0:T(8,128)(2,1)S(1)} %copy-done.18, bf16[3,192,512]{2,1,0:T(8,128)(2,1)} %collective-permute-done.2.refs_3_, ...), custom_call_target="tpu_custom_call" | custom-call | flops 1000000 | bytes 100000 | tf_op jit(solution)/shard_map/grad_fc/turn/pallas_call | solution.py:291
  94.5 2.2 %copy-done.9 = bf16[3,512,1536]{2,1,0:T(8,128)(2,1)} copy-done((bf16[3,512,1536]{2,1,0:T(8,128)(2,1)}, bf16[3,512,1536]{2,1,0:T(8,128)(2,1)S(1)}, u32[]{:S(2)}) %copy-start.9) | copy-done | bytes 4718616
  98.0 14.1 %all-to-all-done.2.parts_ref = bf16[8,96,1024]{2,1,0:T(8,128)(2,1)S(1)} async-done(((bf16[8,96,1024]{2,1,0:T(8,128)(2,1)}), bf16[8,96,1024]{2,1,0:T(8,128)(2,1)S(1)}, u32[]{:S(2)}, u32[]{:S(2)}) %all-to-all-start.2) | async-done | bytes 1572896 | tf_op jit(solution)/shard_map/unite/all_to_all | solution.py:32
  113.6 3.6 %all-to-all-start.3 = ((bf16[8,128,1024]{2,1,0:T(8,128)(2,1)}), bf16[8,128,1024]{2,1,0:T(8,128)(2,1)S(1)}, u32[]{:S(2)}, u32[]{:S(2)}) async-start(bf16[8,128,1024]{2,1,0:T(8,128)(2,1)} %copy-done.7), calls=%async_computation.3 | async-start | bytes 4194304 | tf_op jit(solution)/shard_map/unite/all_to_all | solution.py:32
  117.3 2.8 %copy-done.21 = bf16[3072,1024]{1,0:T(8,128)(2,1)S(1)} copy-done((bf16[3072,1024]{1,0:T(8,128)(2,1)S(1)}, bf16[3072,1024]{1,0:T(8,128)(2,1)}, u32[]{:S(2)}) %copy-start.21) | copy-done | bytes 6291480
  120.1 11.4 %take_rows.5.cots_ref.refs_3_ = bf16[1536,1024]{1,0:T(8,128)(2,1)S(1)} custom-call(s32[1,1536]{1,0:T(1,128)S(1)} %add.297.position_ref, s32[1,1536]{1,0:T(1,128)S(1)} %get-tuple-element.68.value_ref, bf16[3072,1024]{1,0:T(8,128)(2,1)S(1)} %copy-done.21), custom_call_target="tpu_custom_call" | custom-call | flops 99999997952 | bytes 1000000000 | tf_op jit(solution)/shard_map/cotangent_rows/take_rows/pallas_call | solution.py:137
  131.5 1.6 copy-done.1
  133.1 14.9 %all-to-all-done.3.rows_ref.own_ref.refs_1_ = bf16[8,128,1024]{2,1,0:T(8,128)(2,1)S(1)} async-done(((bf16[8,128,1024]{2,1,0:T(8,128)(2,1)}), bf16[8,128,1024]{2,1,0:T(8,128)(2,1)S(1)}, u32[]{:S(2)}, u32[]{:S(2)}) %all-to-all-start.3) | async-done | bytes 2097184 | tf_op jit(solution)/shard_map/unite/all_to_all | solution.py:32
  148.1 1.9 copy-done.2
  152.2 2.1 %partial_sums.1 = f32[8,9,2,192]{3,2,1,0:T(2,128)} custom-call(s32[8]{0:T(128)S(1)} %broadcast_select_fusion.2.order_ref, f32[4,2,192]{2,1,0:T(2,128)S(1)} %half_sums.1.sums_ref, bf16[8,128,1024]{2,1,0:T(8,128)(2,1)S(1)} %all-to-all-done.3.rows_ref.own_ref.refs_1_, bf16[8,128,1024]{2,1,0:T(8,128)(2,1)S(1)} %collective-permute-done.11.other_ref.refs_2_, ...), custom_call_target="tpu_custom_call" | custom-call | flops 1000000 | bytes 100000 | tf_op jit(solution)/shard_map/norms/partial_sums/pallas_call | solution.py:264
  154.4 6.7 %all-to-all-start.4 = ((f32[8,9,2,192]{3,2,1,0:T(2,128)}), f32[8,9,2,192]{3,2,1,0:T(2,128)S(1)}, u32[]{:S(2)}, u32[]{:S(2)}) async-start(f32[8,9,2,192]{3,2,1,0:T(2,128)} %partial_sums.1), calls=%async_computation.4 | async-start | bytes 294912 | tf_op jit(solution)/shard_map/norms/all_to_all | solution.py:586
  164.2 5.0 %all-to-all-done.4.totals_ref.refs_5_ = f32[8,9,2,192]{3,2,1,0:T(2,128)S(1)} async-done(((f32[8,9,2,192]{3,2,1,0:T(2,128)}), f32[8,9,2,192]{3,2,1,0:T(2,128)S(1)}, u32[]{:S(2)}, u32[]{:S(2)}) %all-to-all-start.4) | async-done | bytes 110624 | tf_op jit(solution)/shard_map/norms/all_to_all | solution.py:586
  170.8 11.0 %weight_gradient.1 = f32[3,512,1024]{2,1,0:T(8,128)} custom-call(s32[8]{0:T(128)S(1)} %broadcast_select_fusion.2.order_ref, s32[1]{0:T(128)} %bitcast.3.which_ref.core_ref, bf16[3,512,1536]{2,1,0:T(8,128)(2,1)} %copy-done.9, bf16[8,128,1024]{2,1,0:T(8,128)(2,1)S(1)} %all-to-all-done.3.rows_ref.own_ref.refs_1_, bf16[8,128,1024]{2,1,0:T(8,128)(2,1)S(1)} %copy-done.6, ...), custom_call_target="tpu_custom_call" | custom-call | flops 99999997952 | bytes 1000000000 | tf_op jit(solution)/shard_map/grad_fc/weight_gradient/pallas_call | solution.py:339
  182.7 1.7 copy.26
  (130 shorter events, 26.3 us)
Async XLA Ops:
  7.2 110.1 %all-gather.2.cloned.1.call-start = ((), (), s32[]{:S(2)}) async-start(), calls=%async_computation.5 | async-start | bytes 6684672 | tf_op jit(solution)/shard_map/gather_cotangents/all_gather | solution.py:443
  7.2 23.5 %collective-permute-start.2 = (bf16[3,192,512]{2,1,0:T(8,128)(2,1)}, bf16[3,192,512]{2,1,0:T(8,128)(2,1)}, u32[]{:S(2)}, u32[]{:S(2)}) collective-permute-start(bf16[3,192,512]{2,1,0:T(8,128)(2,1)} %bitcast.32), channel_id=1, source_target_pairs={{0,64},{16,80},{32,96},{48,112},{64,0},{80,16},{96,32},{112,48},{1... | collective-permute-start | bytes 1769480 | tf_op jit(solution)/shard_map/gather_features/ppermute | solution.py:455
  10.6 20.2 %collective-permute-start.1 = (bf16[3,192,512]{2,1,0:T(8,128)(2,1)}, bf16[3,192,512]{2,1,0:T(8,128)(2,1)S(1)}, u32[]{:S(2)}, u32[]{:S(2)}) collective-permute-start(bf16[3,192,512]{2,1,0:T(8,128)(2,1)} %bitcast.33), channel_id=1, source_target_pairs={{0,48},{16,0},{32,16},{48,32},{64,112},{80,64},{96,80},{112,96},{1... | collective-permute-start | bytes 1769480 | tf_op jit(solution)/shard_map/gather_features/ppermute | solution.py:454
  14.6 16.1 %collective-permute-start = (bf16[3,192,512]{2,1,0:T(8,128)(2,1)}, bf16[3,192,512]{2,1,0:T(8,128)(2,1)}, u32[]{:S(2)}, u32[]{:S(2)}) collective-permute-start(bf16[3,192,512]{2,1,0:T(8,128)(2,1)} %bitcast.34), channel_id=1, source_target_pairs={{0,16},{16,32},{32,48},{48,0},{64,80},{80,96},{96,112},{112,64},{1... | collective-permute-start | bytes 1769480 | tf_op jit(solution)/shard_map/gather_features/ppermute | solution.py:453
  16.6 14.1 %all-to-all-start = ((s32[8,1,192]{2,1,0:T(1,128)}), s32[8,1,192]{2,1,0:T(1,128)S(1)}, u32[]{:S(2)}, u32[]{:S(2)}) async-start(s32[8,1,192]{2,1,0:T(1,128)} %broadcast_in_dim.45), calls=%async_computation | async-start | bytes 16384 | tf_op jit(solution)/shard_map/row_codes/all_to_all | solution.py:449
  32.5 17.3 %collective-permute-start.4 = (bf16[3,192,512]{2,1,0:T(8,128)(2,1)}, bf16[3,192,512]{2,1,0:T(8,128)(2,1)}, u32[]{:S(2)}, u32[]{:S(2)}) collective-permute-start(bf16[3,192,512]{2,1,0:T(8,128)(2,1)} %collective-permute-done.2.refs_3_), channel_id=1, source_target_pairs={{0,48},{16,0},{32,16},{48,32},{64,112},{80,64},{96,80},{112,96},{1... | collective-permute-start | bytes 1769480 | tf_op jit(solution)/shard_map/gather_features/ppermute | solution.py:461
  32.8 17.8 %collective-permute-start.3 = (bf16[3,192,512]{2,1,0:T(8,128)(2,1)}, bf16[3,192,512]{2,1,0:T(8,128)(2,1)}, u32[]{:S(2)}, u32[]{:S(2)}) collective-permute-start(bf16[3,192,512]{2,1,0:T(8,128)(2,1)} %collective-permute-done.2.refs_3_), channel_id=1, source_target_pairs={{0,16},{16,32},{32,48},{48,0},{64,80},{80,96},{96,112},{112,64},{1... | collective-permute-start | bytes 1769480 | tf_op jit(solution)/shard_map/gather_features/ppermute | solution.py:460
  36.4 31.4 %collective-permute-start.7 = (bf16[3,192,512]{2,1,0:T(8,128)(2,1)}, bf16[3,192,512]{2,1,0:T(8,128)(2,1)}, u32[]{:S(2)}, u32[]{:S(2)}) collective-permute-start(bf16[3,192,512]{2,1,0:T(8,128)(2,1)} %collective-permute-done.refs_1_), channel_id=1, source_target_pairs={{0,16},{16,32},{32,48},{48,0},{64,80},{80,96},{96,112},{112,64},{1... | collective-permute-start | bytes 1769480 | tf_op jit(solution)/shard_map/gather_features/ppermute | solution.py:462
  43.5 4.9 %collective-permute-start.5 = (bf16[896,1024]{1,0:T(8,128)(2,1)S(1)}, bf16[896,1024]{1,0:T(8,128)(2,1)S(1)}, u32[]{:S(2)}, u32[]{:S(2)}) collective-permute-start(bf16[896,1024]{1,0:T(8,128)(2,1)S(1)} %take_rows.3), channel_id=1, source_target_pairs={{0,1},{1,0},{2,3},{3,2},{4,5},{5,4},{6,7},{7,6},{8,9},{9,8},{10,11... | collective-permute-start | bytes 5505032 | tf_op jit(solution)/shard_map/embeds/ppermute | solution.py:41
  49.8 8.0 %copy-start = (bf16[3,512,1024]{2,1,0:T(8,128)(2,1)S(1)}, bf16[3,512,1024]{2,1,0:T(8,128)(2,1)}, u32[]{:S(2)}) copy-start(bf16[3,512,1024]{2,1,0:T(8,128)(2,1)} %param.13) | copy-start | bytes 9437188
  50.6 32.3 %all-to-all-start.1 = ((bf16[8,112,1024]{2,1,0:T(8,128)(2,1)}), bf16[8,112,1024]{2,1,0:T(8,128)(2,1)}, u32[]{:S(2)}, u32[]{:S(2)}) async-start(bf16[8,112,1024]{2,1,0:T(8,128)(2,1)} %bitcast.31), calls=%async_computation.1 | async-start | bytes 3670016 | tf_op jit(solution)/shard_map/embeds/all_to_all | solution.py:32
  55.1 16.2 %collective-permute-start.6 = (bf16[3,192,512]{2,1,0:T(8,128)(2,1)}, bf16[3,192,512]{2,1,0:T(8,128)(2,1)}, u32[]{:S(2)}, u32[]{:S(2)}) collective-permute-start(bf16[3,192,512]{2,1,0:T(8,128)(2,1)} %collective-permute-done.4.refs_1_.refs_5_), channel_id=1, source_target_pairs={{0,48},{16,0},{32,16},{48,32},{64,112},{80,64},{96,80},{112,96},{1... | collective-permute-start | bytes 1769480 | tf_op jit(solution)/shard_map/gather_features/ppermute | solution.py:522
  59.9 3.8 %copy-start.13 = (bf16[192,3,512]{2,0,1:T(8,128)(2,1)S(1)}, bf16[192,3,512]{2,0,1:T(8,128)(2,1)}, u32[]{:S(2)}) copy-start(bf16[192,3,512]{2,0,1:T(8,128)(2,1)} %param.9) | copy-start | bytes 1769476
  59.9 3.8 %copy-start.17 = (bf16[3,192,512]{2,1,0:T(8,128)(2,1)S(1)}, bf16[3,192,512]{2,1,0:T(8,128)(2,1)}, u32[]{:S(2)}) copy-start(bf16[3,192,512]{2,1,0:T(8,128)(2,1)} %copy-done.15) | copy-start | bytes 1769476
  63.6 15.5 %collective-permute-start.8 = (bf16[384,1024]{1,0:T(8,128)(2,1)}, bf16[384,1024]{1,0:T(8,128)(2,1)}, u32[]{:S(2)}, u32[]{:S(2)}) collective-permute-start(bf16[384,1024]{1,0:T(8,128)(2,1)} %project.5), channel_id=1, source_target_pairs={{0,1},{1,0},{2,3},{3,2},{4,5},{5,4},{6,7},{7,6},{8,9},{9,8},{10,11... | collective-permute-start | bytes 2359304 | tf_op jit(solution)/shard_map/unite_first/ppermute | solution.py:41
  67.8 7.4 %copy-start.28 = (s32[8]{0:T(128)S(1)}, s32[8]{0:T(128)}, u32[]{:S(2)}) copy-start(s32[8]{0:T(128)} %stack.65) | copy-start | bytes 100
  67.8 7.4 %copy-start.29 = (s32[8]{0:T(128)S(1)}, s32[8]{0:T(128)}, u32[]{:S(2)}) copy-start(s32[8]{0:T(128)} %stack.64) | copy-start | bytes 100
  67.8 7.5 %copy-start.24 = (s32[16,16]{1,0:T(8,128)S(1)}, s32[16,16]{1,0:T(8,128)}, u32[]{:S(2)}) copy-start(s32[16,16]{1,0:T(8,128)} %copy-done.23) | copy-start | bytes 3076
  67.8 7.5 %copy-start.26 = (s32[16,16]{1,0:T(8,128)S(1)}, s32[16,16]{1,0:T(8,128)}, u32[]{:S(2)}) copy-start(s32[16,16]{1,0:T(8,128)} %copy-done.25) | copy-start | bytes 3076
  75.2 3.9 %collective-permute-start.9 = (bf16[384,1024]{1,0:T(8,128)(2,1)}, bf16[384,1024]{1,0:T(8,128)(2,1)}, u32[]{:S(2)}, u32[]{:S(2)}) collective-permute-start(bf16[384,1024]{1,0:T(8,128)(2,1)} %project.6), channel_id=1, source_target_pairs={{0,1},{1,0},{2,3},{3,2},{4,5},{5,4},{6,7},{7,6},{8,9},{9,8},{10,11... | collective-permute-start | bytes 2359304 | tf_op jit(solution)/shard_map/unite_second/ppermute | solution.py:41
  75.9 3.2 %copy-start.11 = (f32[384,1024]{1,0:T(8,128)S(1)}, f32[384,1024]{1,0:T(8,128)}, u32[]{:S(2)}) copy-start(f32[384,1024]{1,0:T(8,128)} %copy-done.10) | copy-start | bytes 4718596
  82.9 29.2 %all-to-all-start.2 = ((bf16[8,96,1024]{2,1,0:T(8,128)(2,1)}), bf16[8,96,1024]{2,1,0:T(8,128)(2,1)S(1)}, u32[]{:S(2)}, u32[]{:S(2)}) async-start(bf16[8,96,1024]{2,1,0:T(8,128)(2,1)} %add_halves.1), calls=%async_computation.2 | async-start | bytes 3145728 | tf_op jit(solution)/shard_map/unite/all_to_all | solution.py:32
  87.3 3.6 %copy-start.14 = (bf16[192,3,512]{2,0,1:T(8,128)(2,1)S(1)}, bf16[192,3,512]{2,0,1:T(8,128)(2,1)}, u32[]{:S(2)}) copy-start(bf16[192,3,512]{2,0,1:T(8,128)(2,1)} %param.9) | copy-start | bytes 1769476
  87.3 3.6 %copy-start.18 = (bf16[3,192,512]{2,1,0:T(8,128)(2,1)S(1)}, bf16[3,192,512]{2,1,0:T(8,128)(2,1)}, u32[]{:S(2)}) copy-start(bf16[3,192,512]{2,1,0:T(8,128)(2,1)} %copy-done.15) | copy-start | bytes 1769476
  90.3 6.4 %collective-permute-start.10 = (bf16[8,12,1024]{2,1,0:T(8,128)(2,1)}, bf16[8,12,1024]{2,1,0:T(8,128)(2,1)}, u32[]{:S(2)}, u32[]{:S(2)}) collective-permute-start(bf16[8,12,1024]{2,1,0:T(8,128)(2,1)} %squeeze.22), channel_id=1, source_target_pairs={{0,1},{1,0},{2,3},{3,2},{4,5},{5,4},{6,7},{7,6},{8,9},{9,8},{10,11... | collective-permute-start | bytes 589832 | tf_op jit(solution)/shard_map/embeds/ppermute | solution.py:41
  113.6 34.4 %all-to-all-start.3 = ((bf16[8,128,1024]{2,1,0:T(8,128)(2,1)}), bf16[8,128,1024]{2,1,0:T(8,128)(2,1)S(1)}, u32[]{:S(2)}, u32[]{:S(2)}) async-start(bf16[8,128,1024]{2,1,0:T(8,128)(2,1)} %copy-done.7), calls=%async_computation.3 | async-start | bytes 4194304 | tf_op jit(solution)/shard_map/unite/all_to_all | solution.py:32
  117.3 2.8 %copy-start.21 = (bf16[3072,1024]{1,0:T(8,128)(2,1)S(1)}, bf16[3072,1024]{1,0:T(8,128)(2,1)}, u32[]{:S(2)}) copy-start(bf16[3072,1024]{1,0:T(8,128)(2,1)} %all-gather.2.cloned.1.call-done.refs_0_) | copy-start | bytes 18874372
  120.1 28.0 %copy-start.19 = (f32[1024]{0:T(1024)S(1)}, f32[1024]{0:T(1024)}, u32[]{:S(2)}) copy-start(f32[1024]{0:T(1024)} %param.16) | copy-start | bytes 12292
  148.1 4.2 %collective-permute-start.11 = (bf16[8,128,1024]{2,1,0:T(8,128)(2,1)S(1)}, bf16[8,128,1024]{2,1,0:T(8,128)(2,1)S(1)}, u32[]{:S(2)}, u32[]{:S(2)}) collective-permute-start(bf16[8,128,1024]{2,1,0:T(8,128)(2,1)S(1)} %all-to-all-done.3.rows_ref.own_ref.refs_1_), channel_id=1, source_target_pairs={{0,1},{1,0},{2,3},{3,2},{4,5},{5,4},{6,7},{7,6},{8,9},{9,8},{10,11... | collective-permute-start | bytes 6291464 | tf_op jit(solution)/shard_map/unite_second/ppermute | solution.py:41
  150.8 10.2 %copy-start.27 = (s32[1536]{0:T(1024)S(1)}, s32[1536]{0:T(1024)}, u32[]{:S(2)}) copy-start(s32[1536]{0:T(1024)} %get-tuple-element.51) | copy-start | bytes 18436
  154.4 14.9 %all-to-all-start.4 = ((f32[8,9,2,192]{3,2,1,0:T(2,128)}), f32[8,9,2,192]{3,2,1,0:T(2,128)S(1)}, u32[]{:S(2)}, u32[]{:S(2)}) async-start(f32[8,9,2,192]{3,2,1,0:T(2,128)} %partial_sums.1), calls=%async_computation.4 | async-start | bytes 294912 | tf_op jit(solution)/shard_map/norms/all_to_all | solution.py:586
  170.8 11.0 %copy-start.20 = (f32[1024]{0:T(1024)S(1)}, f32[1024]{0:T(1024)}, u32[]{:S(2)}) copy-start(f32[1024]{0:T(1024)} %param.15) | copy-start | bytes 12292
  (16 other events, 24.9 us)
Sparse Core Ops, SparseCore 0:
  14.8 41.7 all-gather.1

commit v3 on v2

--- a/solution.py
+++ b/solution.py
@@ -310,7 +310,7 @@
         united_refs = refs[1:3]
         turned_ref, cots_ref, gain_ref, totals_ref, out_ref, g_ref = refs[:1] + refs[3:]
 
-        @pl.when(pl.program_id(0) == 0)
+        @pl.when((pl.program_id(0) == 0) & (pl.program_id(1) == 0))
         def _():
             for place in range(REPLICAS):
                 both = totals_ref[0, order_ref[place]]
@@ -338,13 +338,13 @@
     smem = pl.BlockSpec(memory_space=pltpu.SMEM)
     return pl.pallas_call(
         kernel,
-        grid=(taps,),
+        grid=(taps, 2),
         out_shape=jax.ShapeDtypeStruct((taps, feat, cols), F32),
         in_specs=[smem, smem]
-        + [pl.BlockSpec((1, feat, rows), lambda t: (t, 0, 0))]
+        + [pl.BlockSpec((1, feat // 2, rows), lambda t, h: (t, h, 0))]
         + [whole(united[0].shape)] * 2
         + [whole((rows, cols)), whole((1, cols)), whole(totals.shape)],
-        out_specs=pl.BlockSpec((1, feat, cols), lambda t: (t, 0, 0)),
+        out_specs=pl.BlockSpec((1, feat // 2, cols), lambda t, h: (t, h, 0)),
         scratch_shapes=[pltpu.VMEM((rows, cols), BF)],
         compiler_params=pltpu.CompilerParams(vmem_limit_bytes=48 * MIB),
         cost_estimate=LONG,

time: 192 us -> 193 us (level)
  no operation moved by 1% of the time
where the time goes in v3:
time: 193 us; the launch traced here: 192 us
  Pallas kernels  58 us (30%)
  waiting for transfers between devices  49 us (25%)
  starting transfers between devices  36.4 us (19%)
  local copies, waits for them, and re-layouts  26 us (13%)
  between operations  15.2 us (8%)
  other arithmetic  5.82 us (3%)
    all_to_all x3, waiting for transfers between devices, to_chips(): return lax.all_to_all(x, 'tensor', 0, 0, axis_index_groups=CHIP_GROUPS)  30 us
    unnamed x61, local copies, waits for them, and re-layouts  22 us
    pallas_call x3, Pallas kernels, take_rows(): pl.pallas_call(kernel, grid=(count // step,), out_shape=jax.ShapeDtypeStr...  20.9 us
    pallas_call x4, Pallas kernels, project(): pl.pallas_call(kernel, out_shape=jax.ShapeDtypeStruct((2 * per_server, co...  13.5 us
    all_to_all x3, starting transfers between devices, to_chips(): return lax.all_to_all(x, 'tensor', 0, 0, axis_index_groups=CHIP_GROUPS)  12.4 us
    pallas_call x1, Pallas kernels, weight_gradient(): pl.pallas_call(kernel, grid=(taps, 2), out_shape=jax.ShapeDtypeStruct((ta...  11.8 us
    all_to_all x1, waiting for transfers between devices, body(): codes = lax.all_to_all(code, 'replica', 0, 0)  8.27 us
    all_to_all x1, starting transfers between devices, body(): totals = lax.all_to_all(message, 'replica', 0, 0)  6.69 us
  transfers between devices with their start and end apart: 18, of which 8 were waited for; matrix products, arithmetic and copies ran while one was open for 6% of the time, Pallas kernels for 23%

profile of v3, /device:TPU:0, one launch (start us, length us, event | category | flops | bytes accessed | tf_op | source)
XLA Modules:
  0.0 192.1 jit_solution(17583024913993142601)
XLA Ops:
  7.2 3.4 %collective-permute-start.2 = (bf16[3,192,512]{2,1,0:T(8,128)(2,1)}, bf16[3,192,512]{2,1,0:T(8,128)(2,1)}, u32[]{:S(2)}, u32[]{:S(2)}) collective-permute-start(bf16[3,192,512]{2,1,0:T(8,128)(2,1)} %bitcast.32), channel_id=1, source_target_pairs={{0,64},{16,80},{32,96},{48,112},{64,0},{80,16},{96,32},{112,48},{1... | collective-permute-start | bytes 1769480 | tf_op jit(solution)/shard_map/gather_features/ppermute | solution.py:455
  10.6 4.0 %collective-permute-start.1 = (bf16[3,192,512]{2,1,0:T(8,128)(2,1)}, bf16[3,192,512]{2,1,0:T(8,128)(2,1)S(1)}, u32[]{:S(2)}, u32[]{:S(2)}) collective-permute-start(bf16[3,192,512]{2,1,0:T(8,128)(2,1)} %bitcast.33), channel_id=1, source_target_pairs={{0,48},{16,0},{32,16},{48,32},{64,112},{80,64},{96,80},{112,96},{1... | collective-permute-start | bytes 1769480 | tf_op jit(solution)/shard_map/gather_features/ppermute | solution.py:454
  16.6 4.5 %all-to-all-start = ((s32[8,1,192]{2,1,0:T(1,128)}), s32[8,1,192]{2,1,0:T(1,128)S(1)}, u32[]{:S(2)}, u32[]{:S(2)}) async-start(s32[8,1,192]{2,1,0:T(1,128)} %broadcast_in_dim.45), calls=%async_computation | async-start | bytes 16384 | tf_op jit(solution)/shard_map/row_codes/all_to_all | solution.py:449
  22.4 8.3 %all-to-all-done = s32[8,1,192]{2,1,0:T(1,128)S(1)} async-done(((s32[8,1,192]{2,1,0:T(1,128)}), s32[8,1,192]{2,1,0:T(1,128)S(1)}, u32[]{:S(2)}, u32[]{:S(2)}) %all-to-all-start) | async-done | bytes 6176 | tf_op jit(solution)/shard_map/row_codes/all_to_all | solution.py:449
  32.8 1.8 collective-permute-start.3
  36.5 2.2 %copy-done.22 = bf16[2000,1024]{1,0:T(8,128)(2,1)S(1)} copy-done((bf16[2000,1024]{1,0:T(8,128)(2,1)S(1)}, bf16[2000,1024]{1,0:T(8,128)(2,1)}, u32[]{:S(2)}) %copy-start.22) | copy-done | bytes 4096024
  38.8 4.8 %take_rows.3 = bf16[896,1024]{1,0:T(8,128)(2,1)S(1)} custom-call(s32[1,1536]{1,0:T(1,128)S(1)} %get-tuple-element.71.position_ref, s32[1,1536]{1,0:T(1,128)S(1)} %get-tuple-element.73.value_ref, bf16[2000,1024]{1,0:T(8,128)(2,1)S(1)} %copy-done.22), custom_call_target="tpu_custom_call" | custom-call | flops 99999997952 | bytes 1000000000 | tf_op jit(solution)/shard_map/embeds/take_rows/pallas_call | solution.py:137
  43.6 4.8 %take_rows.4.a_ref = bf16[896,1024]{1,0:T(8,128)(2,1)S(1)} custom-call(s32[1,1536]{1,0:T(1,128)S(1)} %compare_select_fusion.1.position_ref, s32[1,1536]{1,0:T(1,128)S(1)} %get-tuple-element.73.value_ref, bf16[2000,1024]{1,0:T(8,128)(2,1)S(1)} %copy-done.22), custom_call_target="tpu_custom_call" | custom-call | flops 99999997952 | bytes 1000000000 | tf_op jit(solution)/shard_map/embeds/take_rows/pallas_call | solution.py:137
  50.6 4.5 %all-to-all-start.1 = ((bf16[8,112,1024]{2,1,0:T(8,128)(2,1)}), bf16[8,112,1024]{2,1,0:T(8,128)(2,1)}, u32[]{:S(2)}, u32[]{:S(2)}) async-start(bf16[8,112,1024]{2,1,0:T(8,128)(2,1)} %bitcast.31), calls=%async_computation.1 | async-start | bytes 3670016 | tf_op jit(solution)/shard_map/embeds/all_to_all | solution.py:32
  55.1 2.7 %collective-permute-start.6 = (bf16[3,192,512]{2,1,0:T(8,128)(2,1)}, bf16[3,192,512]{2,1,0:T(8,128)(2,1)}, u32[]{:S(2)}, u32[]{:S(2)}) collective-permute-start(bf16[3,192,512]{2,1,0:T(8,128)(2,1)} %collective-permute-done.4.refs_1_.refs_5_), channel_id=1, source_target_pairs={{0,48},{16,0},{32,16},{48,32},{64,112},{80,64},{96,80},{112,96},{1... | collective-permute-start | bytes 1769480 | tf_op jit(solution)/shard_map/gather_features/ppermute | solution.py:522
  59.9 3.6 %project.5 = bf16[384,1024]{1,0:T(8,128)(2,1)} custom-call(s32[1]{0:T(128)} %bitcast.5.which_ref, bf16[3,192,512]{2,1,0:T(8,128)(2,1)S(1)} %bitcast.35, bf16[3,192,512]{2,1,0:T(8,128)(2,1)} %collective-permute-done.refs_1_, bf16[3,192,512]{2,1,0:T(8,128)(2,1)S(1)} %copy-done.16, bf16[3,192,512]{2,1,0:T(8,128)(2,1)} %collective-permute-done.2.refs_3_, ...), custom_call_target="tpu_custom_call" | custom-call | flops 99999997952 | bytes 1000000000 | tf_op jit(solution)/shard_map/unite_first/project/pallas_call | solution.py:83
  63.7 2.8 %project.4.k0 = f32[384,1024]{1,0:T(8,128)S(1)} custom-call(s32[1]{0:T(128)} %bitcast.3.which_ref.core_ref, bf16[3,192,512]{2,1,0:T(8,128)(2,1)S(1)} %bitcast.36, bf16[3,192,512]{2,1,0:T(8,128)(2,1)} %collective-permute-done.refs_1_, bf16[3,192,512]{2,1,0:T(8,128)(2,1)S(1)} %copy-done.17, bf16[3,192,512]{2,1,0:T(8,128)(2,1)} %collective-permute-done.2.refs_3_, ...), custom_call_target="tpu_custom_call" | custom-call | flops 99999997952 | bytes 1000000000 | tf_op jit(solution)/shard_map/unite_first/project/pallas_call | solution.py:83
  67.8 3.5 %collective-permute-done.6.refs_3_.refs_7_ = bf16[3,192,512]{2,1,0:T(8,128)(2,1)} collective-permute-done((bf16[3,192,512]{2,1,0:T(8,128)(2,1)}, bf16[3,192,512]{2,1,0:T(8,128)(2,1)}, u32[]{:S(2)}, u32[]{:S(2)}) %collective-permute-start.6) | collective-permute-done | bytes 589856 | tf_op jit(solution)/shard_map/gather_features/ppermute | solution.py:522
  71.3 3.9 %project.6 = bf16[384,1024]{1,0:T(8,128)(2,1)} custom-call(s32[1]{0:T(128)} %bitcast.5.which_ref, bf16[3,192,512]{2,1,0:T(8,128)(2,1)} %collective-permute-done.3.refs_0_.refs_4_, bf16[3,192,512]{2,1,0:T(8,128)(2,1)} %collective-permute-done.4.refs_1_.refs_5_, bf16[3,192,512]{2,1,0:T(8,128)(2,1)} %collective-permute-done.7.refs_2_.refs_6_, ...), custom_call_target="tpu_custom_call" | custom-call | flops 1000000 | bytes 100000 | tf_op jit(solution)/shard_map/unite_second/project/pallas_call | solution.py:83
  75.9 3.1 %project.7.k1 = f32[384,1024]{1,0:T(8,128)S(1)} custom-call(s32[1]{0:T(128)} %bitcast.3.which_ref.core_ref, bf16[3,192,512]{2,1,0:T(8,128)(2,1)} %collective-permute-done.3.refs_0_.refs_4_, bf16[3,192,512]{2,1,0:T(8,128)(2,1)} %collective-permute-done.4.refs_1_.refs_5_, bf16[3,192,512]{2,1,0:T(8,128)(2,1)} %collective-permute-done.7.refs_2_.refs_6_, ...), custom_call_target="tpu_custom_call" | custom-call | flops 1000000 | bytes 100000 | tf_op jit(solution)/shard_map/unite_second/project/pallas_call | solution.py:83
  79.1 2.8 %add_halves.1 = bf16[8,96,1024]{2,1,0:T(8,128)(2,1)} custom-call(f32[384,1024]{1,0:T(8,128)S(1)} %copy-done.11, bf16[384,1024]{1,0:T(8,128)(2,1)} %collective-permute-done.8.r0, f32[384,1024]{1,0:T(8,128)S(1)} %project.7.k1, bf16[384,1024]{1,0:T(8,128)(2,1)} %collective-permute-done.9.r1), custom_call_target="tpu_custom_call" | custom-call | flops 1000000 | bytes 100000 | tf_op jit(solution)/shard_map/unite_second/add_halves/pallas_call | solution.py:161
  82.9 4.3 %all-to-all-start.2 = ((bf16[8,96,1024]{2,1,0:T(8,128)(2,1)}), bf16[8,96,1024]{2,1,0:T(8,128)(2,1)S(1)}, u32[]{:S(2)}, u32[]{:S(2)}) async-start(bf16[8,96,1024]{2,1,0:T(8,128)(2,1)} %add_halves.1), calls=%async_computation.2 | async-start | bytes 3145728 | tf_op jit(solution)/shard_map/unite/all_to_all | solution.py:32
  87.3 1.9 %reduce_sum.54 = bf16[112,1024]{1,0:T(8,128)(2,1)S(1)} reduce(bf16[8,112,1024]{2,1,0:T(8,128)(2,1)} %all-to-all-done.1, bf16[]{:T(256)} %constant.166.clone.1), dimensions={0}, to_apply=%region_4.5 | reduce | flops 802816 | bytes 2064386 | tf_op jit(solution)/shard_map/embeds/reduce_sum | solution.py:548
  90.9 3.7 %turn.1.refs_0_ = bf16[3,512,1536]{2,1,0:T(8,128)(2,1)S(1)} custom-call(bf16[3,192,512]{2,1,0:T(8,128)(2,1)S(1)} %bitcast.37, bf16[3,192,512]{2,1,0:T(8,128)(2,1)} %collective-permute-done.refs_1_, bf16[3,192,512]{2,1,0:T(8,128)(2,1)S(1)} %copy-done.18, bf16[3,192,512]{2,1,0:T(8,128)(2,1)} %collective-permute-done.2.refs_3_, ...), custom_call_target="tpu_custom_call" | custom-call | flops 1000000 | bytes 100000 | tf_op jit(solution)/shard_map/grad_fc/turn/pallas_call | solution.py:291
  94.5 2.2 %copy-done.9 = bf16[3,512,1536]{2,1,0:T(8,128)(2,1)} copy-done((bf16[3,512,1536]{2,1,0:T(8,128)(2,1)}, bf16[3,512,1536]{2,1,0:T(8,128)(2,1)S(1)}, u32[]{:S(2)}) %copy-start.9) | copy-done | bytes 4718616
  98.0 14.1 %all-to-all-done.2.parts_ref = bf16[8,96,1024]{2,1,0:T(8,128)(2,1)S(1)} async-done(((bf16[8,96,1024]{2,1,0:T(8,128)(2,1)}), bf16[8,96,1024]{2,1,0:T(8,128)(2,1)S(1)}, u32[]{:S(2)}, u32[]{:S(2)}) %all-to-all-start.2) | async-done | bytes 1572896 | tf_op jit(solution)/shard_map/unite/all_to_all | solution.py:32
  113.6 3.6 %all-to-all-start.3 = ((bf16[8,128,1024]{2,1,0:T(8,128)(2,1)}), bf16[8,128,1024]{2,1,0:T(8,128)(2,1)S(1)}, u32[]{:S(2)}, u32[]{:S(2)}) async-start(bf16[8,128,1024]{2,1,0:T(8,128)(2,1)} %copy-done.7), calls=%async_computation.3 | async-start | bytes 4194304 | tf_op jit(solution)/shard_map/unite/all_to_all | solution.py:32
  117.3 2.8 %copy-done.21 = bf16[3072,1024]{1,0:T(8,128)(2,1)S(1)} copy-done((bf16[3072,1024]{1,0:T(8,128)(2,1)S(1)}, bf16[3072,1024]{1,0:T(8,128)(2,1)}, u32[]{:S(2)}) %copy-start.21) | copy-done | bytes 6291480
  120.1 11.4 %take_rows.5.cots_ref.refs_3_ = bf16[1536,1024]{1,0:T(8,128)(2,1)S(1)} custom-call(s32[1,1536]{1,0:T(1,128)S(1)} %add.297.position_ref, s32[1,1536]{1,0:T(1,128)S(1)} %get-tuple-element.68.value_ref, bf16[3072,1024]{1,0:T(8,128)(2,1)S(1)} %copy-done.21), custom_call_target="tpu_custom_call" | custom-call | flops 99999997952 | bytes 1000000000 | tf_op jit(solution)/shard_map/cotangent_rows/take_rows/pallas_call | solution.py:137
  131.5 1.6 copy-done.1
  133.1 14.9 %all-to-all-done.3.rows_ref.own_ref.refs_1_ = bf16[8,128,1024]{2,1,0:T(8,128)(2,1)S(1)} async-done(((bf16[8,128,1024]{2,1,0:T(8,128)(2,1)}), bf16[8,128,1024]{2,1,0:T(8,128)(2,1)S(1)}, u32[]{:S(2)}, u32[]{:S(2)}) %all-to-all-start.3) | async-done | bytes 2097184 | tf_op jit(solution)/shard_map/unite/all_to_all | solution.py:32
  148.1 1.9 copy-done.2
  152.2 2.1 %partial_sums.1 = f32[8,9,2,192]{3,2,1,0:T(2,128)} custom-call(s32[8]{0:T(128)S(1)} %broadcast_select_fusion.2.order_ref, f32[4,2,192]{2,1,0:T(2,128)S(1)} %half_sums.1.sums_ref, bf16[8,128,1024]{2,1,0:T(8,128)(2,1)S(1)} %all-to-all-done.3.rows_ref.own_ref.refs_1_, bf16[8,128,1024]{2,1,0:T(8,128)(2,1)S(1)} %collective-permute-done.11.other_ref.refs_2_, ...), custom_call_target="tpu_custom_call" | custom-call | flops 1000000 | bytes 100000 | tf_op jit(solution)/shard_map/norms/partial_sums/pallas_call | solution.py:264
  154.4 6.7 %all-to-all-start.4 = ((f32[8,9,2,192]{3,2,1,0:T(2,128)}), f32[8,9,2,192]{3,2,1,0:T(2,128)S(1)}, u32[]{:S(2)}, u32[]{:S(2)}) async-start(f32[8,9,2,192]{3,2,1,0:T(2,128)} %partial_sums.1), calls=%async_computation.4 | async-start | bytes 294912 | tf_op jit(solution)/shard_map/norms/all_to_all | solution.py:586
  164.2 5.0 %all-to-all-done.4.totals_ref.refs_5_ = f32[8,9,2,192]{3,2,1,0:T(2,128)S(1)} async-done(((f32[8,9,2,192]{3,2,1,0:T(2,128)}), f32[8,9,2,192]{3,2,1,0:T(2,128)S(1)}, u32[]{:S(2)}, u32[]{:S(2)}) %all-to-all-start.4) | async-done | bytes 110624 | tf_op jit(solution)/shard_map/norms/all_to_all | solution.py:586
  170.8 11.8 %weight_gradient.1 = f32[3,512,1024]{2,1,0:T(8,128)} custom-call(s32[8]{0:T(128)S(1)} %broadcast_select_fusion.2.order_ref, s32[1]{0:T(128)} %bitcast.3.which_ref.core_ref, bf16[3,512,1536]{2,1,0:T(8,128)(2,1)} %copy-done.9, bf16[8,128,1024]{2,1,0:T(8,128)(2,1)S(1)} %all-to-all-done.3.rows_ref.own_ref.refs_1_, bf16[8,128,1024]{2,1,0:T(8,128)(2,1)S(1)} %copy-done.6, ...), custom_call_target="tpu_custom_call" | custom-call | flops 99999997952 | bytes 1000000000 | tf_op jit(solution)/shard_map/grad_fc/weight_gradient/pallas_call | solution.py:339
  183.5 1.7 copy.26
  (130 shorter events, 26.3 us)
Async XLA Ops:
  7.2 110.1 %all-gather.2.cloned.1.call-start = ((), (), s32[]{:S(2)}) async-start(), calls=%async_computation.5 | async-start | bytes 6684672 | tf_op jit(solution)/shard_map/gather_cotangents/all_gather | solution.py:443
  7.2 23.5 %collective-permute-start.2 = (bf16[3,192,512]{2,1,0:T(8,128)(2,1)}, bf16[3,192,512]{2,1,0:T(8,128)(2,1)}, u32[]{:S(2)}, u32[]{:S(2)}) collective-permute-start(bf16[3,192,512]{2,1,0:T(8,128)(2,1)} %bitcast.32), channel_id=1, source_target_pairs={{0,64},{16,80},{32,96},{48,112},{64,0},{80,16},{96,32},{112,48},{1... | collective-permute-start | bytes 1769480 | tf_op jit(solution)/shard_map/gather_features/ppermute | solution.py:455
  10.6 20.2 %collective-permute-start.1 = (bf16[3,192,512]{2,1,0:T(8,128)(2,1)}, bf16[3,192,512]{2,1,0:T(8,128)(2,1)S(1)}, u32[]{:S(2)}, u32[]{:S(2)}) collective-permute-start(bf16[3,192,512]{2,1,0:T(8,128)(2,1)} %bitcast.33), channel_id=1, source_target_pairs={{0,48},{16,0},{32,16},{48,32},{64,112},{80,64},{96,80},{112,96},{1... | collective-permute-start | bytes 1769480 | tf_op jit(solution)/shard_map/gather_features/ppermute | solution.py:454
  14.6 16.1 %collective-permute-start = (bf16[3,192,512]{2,1,0:T(8,128)(2,1)}, bf16[3,192,512]{2,1,0:T(8,128)(2,1)}, u32[]{:S(2)}, u32[]{:S(2)}) collective-permute-start(bf16[3,192,512]{2,1,0:T(8,128)(2,1)} %bitcast.34), channel_id=1, source_target_pairs={{0,16},{16,32},{32,48},{48,0},{64,80},{80,96},{96,112},{112,64},{1... | collective-permute-start | bytes 1769480 | tf_op jit(solution)/shard_map/gather_features/ppermute | solution.py:453
  16.6 14.1 %all-to-all-start = ((s32[8,1,192]{2,1,0:T(1,128)}), s32[8,1,192]{2,1,0:T(1,128)S(1)}, u32[]{:S(2)}, u32[]{:S(2)}) async-start(s32[8,1,192]{2,1,0:T(1,128)} %broadcast_in_dim.45), calls=%async_computation | async-start | bytes 16384 | tf_op jit(solution)/shard_map/row_codes/all_to_all | solution.py:449
  32.5 17.3 %collective-permute-start.4 = (bf16[3,192,512]{2,1,0:T(8,128)(2,1)}, bf16[3,192,512]{2,1,0:T(8,128)(2,1)}, u32[]{:S(2)}, u32[]{:S(2)}) collective-permute-start(bf16[3,192,512]{2,1,0:T(8,128)(2,1)} %collective-permute-done.2.refs_3_), channel_id=1, source_target_pairs={{0,48},{16,0},{32,16},{48,32},{64,112},{80,64},{96,80},{112,96},{1... | collective-permute-start | bytes 1769480 | tf_op jit(solution)/shard_map/gather_features/ppermute | solution.py:461
  32.8 17.8 %collective-permute-start.3 = (bf16[3,192,512]{2,1,0:T(8,128)(2,1)}, bf16[3,192,512]{2,1,0:T(8,128)(2,1)}, u32[]{:S(2)}, u32[]{:S(2)}) collective-permute-start(bf16[3,192,512]{2,1,0:T(8,128)(2,1)} %collective-permute-done.2.refs_3_), channel_id=1, source_target_pairs={{0,16},{16,32},{32,48},{48,0},{64,80},{80,96},{96,112},{112,64},{1... | collective-permute-start | bytes 1769480 | tf_op jit(solution)/shard_map/gather_features/ppermute | solution.py:460
  36.4 31.4 %collective-permute-start.7 = (bf16[3,192,512]{2,1,0:T(8,128)(2,1)}, bf16[3,192,512]{2,1,0:T(8,128)(2,1)}, u32[]{:S(2)}, u32[]{:S(2)}) collective-permute-start(bf16[3,192,512]{2,1,0:T(8,128)(2,1)} %collective-permute-done.refs_1_), channel_id=1, source_target_pairs={{0,16},{16,32},{32,48},{48,0},{64,80},{80,96},{96,112},{112,64},{1... | collective-permute-start | bytes 1769480 | tf_op jit(solution)/shard_map/gather_features/ppermute | solution.py:462
  43.5 4.9 %collective-permute-start.5 = (bf16[896,1024]{1,0:T(8,128)(2,1)S(1)}, bf16[896,1024]{1,0:T(8,128)(2,1)S(1)}, u32[]{:S(2)}, u32[]{:S(2)}) collective-permute-start(bf16[896,1024]{1,0:T(8,128)(2,1)S(1)} %take_rows.3), channel_id=1, source_target_pairs={{0,1},{1,0},{2,3},{3,2},{4,5},{5,4},{6,7},{7,6},{8,9},{9,8},{10,11... | collective-permute-start | bytes 5505032 | tf_op jit(solution)/shard_map/embeds/ppermute | solution.py:41
  49.8 8.0 %copy-start = (bf16[3,512,1024]{2,1,0:T(8,128)(2,1)S(1)}, bf16[3,512,1024]{2,1,0:T(8,128)(2,1)}, u32[]{:S(2)}) copy-start(bf16[3,512,1024]{2,1,0:T(8,128)(2,1)} %param.13) | copy-start | bytes 9437188
  50.6 32.3 %all-to-all-start.1 = ((bf16[8,112,1024]{2,1,0:T(8,128)(2,1)}), bf16[8,112,1024]{2,1,0:T(8,128)(2,1)}, u32[]{:S(2)}, u32[]{:S(2)}) async-start(bf16[8,112,1024]{2,1,0:T(8,128)(2,1)} %bitcast.31), calls=%async_computation.1 | async-start | bytes 3670016 | tf_op jit(solution)/shard_map/embeds/all_to_all | solution.py:32
  55.1 16.2 %collective-permute-start.6 = (bf16[3,192,512]{2,1,0:T(8,128)(2,1)}, bf16[3,192,512]{2,1,0:T(8,128)(2,1)}, u32[]{:S(2)}, u32[]{:S(2)}) collective-permute-start(bf16[3,192,512]{2,1,0:T(8,128)(2,1)} %collective-permute-done.4.refs_1_.refs_5_), channel_id=1, source_target_pairs={{0,48},{16,0},{32,16},{48,32},{64,112},{80,64},{96,80},{112,96},{1... | collective-permute-start | bytes 1769480 | tf_op jit(solution)/shard_map/gather_features/ppermute | solution.py:522
  59.9 3.8 %copy-start.13 = (bf16[192,3,512]{2,0,1:T(8,128)(2,1)S(1)}, bf16[192,3,512]{2,0,1:T(8,128)(2,1)}, u32[]{:S(2)}) copy-start(bf16[192,3,512]{2,0,1:T(8,128)(2,1)} %param.9) | copy-start | bytes 1769476
  59.9 3.8 %copy-start.17 = (bf16[3,192,512]{2,1,0:T(8,128)(2,1)S(1)}, bf16[3,192,512]{2,1,0:T(8,128)(2,1)}, u32[]{:S(2)}) copy-start(bf16[3,192,512]{2,1,0:T(8,128)(2,1)} %copy-done.15) | copy-start | bytes 1769476
  63.6 15.5 %collective-permute-start.8 = (bf16[384,1024]{1,0:T(8,128)(2,1)}, bf16[384,1024]{1,0:T(8,128)(2,1)}, u32[]{:S(2)}, u32[]{:S(2)}) collective-permute-start(bf16[384,1024]{1,0:T(8,128)(2,1)} %project.5), channel_id=1, source_target_pairs={{0,1},{1,0},{2,3},{3,2},{4,5},{5,4},{6,7},{7,6},{8,9},{9,8},{10,11... | collective-permute-start | bytes 2359304 | tf_op jit(solution)/shard_map/unite_first/ppermute | solution.py:41
  67.8 7.4 %copy-start.28 = (s32[8]{0:T(128)S(1)}, s32[8]{0:T(128)}, u32[]{:S(2)}) copy-start(s32[8]{0:T(128)} %stack.65) | copy-start | bytes 100
  67.8 7.4 %copy-start.29 = (s32[8]{0:T(128)S(1)}, s32[8]{0:T(128)}, u32[]{:S(2)}) copy-start(s32[8]{0:T(128)} %stack.64) | copy-start | bytes 100
  67.8 7.5 %copy-start.24 = (s32[16,16]{1,0:T(8,128)S(1)}, s32[16,16]{1,0:T(8,128)}, u32[]{:S(2)}) copy-start(s32[16,16]{1,0:T(8,128)} %copy-done.23) | copy-start | bytes 3076
  67.8 7.5 %copy-start.26 = (s32[16,16]{1,0:T(8,128)S(1)}, s32[16,16]{1,0:T(8,128)}, u32[]{:S(2)}) copy-start(s32[16,16]{1,0:T(8,128)} %copy-done.25) | copy-start | bytes 3076
  75.2 3.9 %collective-permute-start.9 = (bf16[384,1024]{1,0:T(8,128)(2,1)}, bf16[384,1024]{1,0:T(8,128)(2,1)}, u32[]{:S(2)}, u32[]{:S(2)}) collective-permute-start(bf16[384,1024]{1,0:T(8,128)(2,1)} %project.6), channel_id=1, source_target_pairs={{0,1},{1,0},{2,3},{3,2},{4,5},{5,4},{6,7},{7,6},{8,9},{9,8},{10,11... | collective-permute-start | bytes 2359304 | tf_op jit(solution)/shard_map/unite_second/ppermute | solution.py:41
  75.9 3.2 %copy-start.11 = (f32[384,1024]{1,0:T(8,128)S(1)}, f32[384,1024]{1,0:T(8,128)}, u32[]{:S(2)}) copy-start(f32[384,1024]{1,0:T(8,128)} %copy-done.10) | copy-start | bytes 4718596
  82.9 29.2 %all-to-all-start.2 = ((bf16[8,96,1024]{2,1,0:T(8,128)(2,1)}), bf16[8,96,1024]{2,1,0:T(8,128)(2,1)S(1)}, u32[]{:S(2)}, u32[]{:S(2)}) async-start(bf16[8,96,1024]{2,1,0:T(8,128)(2,1)} %add_halves.1), calls=%async_computation.2 | async-start | bytes 3145728 | tf_op jit(solution)/shard_map/unite/all_to_all | solution.py:32
  87.3 3.6 %copy-start.14 = (bf16[192,3,512]{2,0,1:T(8,128)(2,1)S(1)}, bf16[192,3,512]{2,0,1:T(8,128)(2,1)}, u32[]{:S(2)}) copy-start(bf16[192,3,512]{2,0,1:T(8,128)(2,1)} %param.9) | copy-start | bytes 1769476
  87.3 3.6 %copy-start.18 = (bf16[3,192,512]{2,1,0:T(8,128)(2,1)S(1)}, bf16[3,192,512]{2,1,0:T(8,128)(2,1)}, u32[]{:S(2)}) copy-start(bf16[3,192,512]{2,1,0:T(8,128)(2,1)} %copy-done.15) | copy-start | bytes 1769476
  90.3 6.4 %collective-permute-start.10 = (bf16[8,12,1024]{2,1,0:T(8,128)(2,1)}, bf16[8,12,1024]{2,1,0:T(8,128)(2,1)}, u32[]{:S(2)}, u32[]{:S(2)}) collective-permute-start(bf16[8,12,1024]{2,1,0:T(8,128)(2,1)} %squeeze.22), channel_id=1, source_target_pairs={{0,1},{1,0},{2,3},{3,2},{4,5},{5,4},{6,7},{7,6},{8,9},{9,8},{10,11... | collective-permute-start | bytes 589832 | tf_op jit(solution)/shard_map/embeds/ppermute | solution.py:41
  113.6 34.4 %all-to-all-start.3 = ((bf16[8,128,1024]{2,1,0:T(8,128)(2,1)}), bf16[8,128,1024]{2,1,0:T(8,128)(2,1)S(1)}, u32[]{:S(2)}, u32[]{:S(2)}) async-start(bf16[8,128,1024]{2,1,0:T(8,128)(2,1)} %copy-done.7), calls=%async_computation.3 | async-start | bytes 4194304 | tf_op jit(solution)/shard_map/unite/all_to_all | solution.py:32
  117.3 2.8 %copy-start.21 = (bf16[3072,1024]{1,0:T(8,128)(2,1)S(1)}, bf16[3072,1024]{1,0:T(8,128)(2,1)}, u32[]{:S(2)}) copy-start(bf16[3072,1024]{1,0:T(8,128)(2,1)} %all-gather.2.cloned.1.call-done.refs_0_) | copy-start | bytes 18874372
  120.1 28.0 %copy-start.19 = (f32[1024]{0:T(1024)S(1)}, f32[1024]{0:T(1024)}, u32[]{:S(2)}) copy-start(f32[1024]{0:T(1024)} %param.16) | copy-start | bytes 12292
  148.1 4.2 %collective-permute-start.11 = (bf16[8,128,1024]{2,1,0:T(8,128)(2,1)S(1)}, bf16[8,128,1024]{2,1,0:T(8,128)(2,1)S(1)}, u32[]{:S(2)}, u32[]{:S(2)}) collective-permute-start(bf16[8,128,1024]{2,1,0:T(8,128)(2,1)S(1)} %all-to-all-done.3.rows_ref.own_ref.refs_1_), channel_id=1, source_target_pairs={{0,1},{1,0},{2,3},{3,2},{4,5},{5,4},{6,7},{7,6},{8,9},{9,8},{10,11... | collective-permute-start | bytes 6291464 | tf_op jit(solution)/shard_map/unite_second/ppermute | solution.py:41
  150.8 10.2 %copy-start.27 = (s32[1536]{0:T(1024)S(1)}, s32[1536]{0:T(1024)}, u32[]{:S(2)}) copy-start(s32[1536]{0:T(1024)} %get-tuple-element.51) | copy-start | bytes 18436
  154.4 14.9 %all-to-all-start.4 = ((f32[8,9,2,192]{3,2,1,0:T(2,128)}), f32[8,9,2,192]{3,2,1,0:T(2,128)S(1)}, u32[]{:S(2)}, u32[]{:S(2)}) async-start(f32[8,9,2,192]{3,2,1,0:T(2,128)} %partial_sums.1), calls=%async_computation.4 | async-start | bytes 294912 | tf_op jit(solution)/shard_map/norms/all_to_all | solution.py:586
  170.8 11.8 %copy-start.20 = (f32[1024]{0:T(1024)S(1)}, f32[1024]{0:T(1024)}, u32[]{:S(2)}) copy-start(f32[1024]{0:T(1024)} %param.15) | copy-start | bytes 12292
  (16 other events, 24.9 us)
Sparse Core Ops, SparseCore 0:
  14.8 41.7 all-gather.1
